TPU v7x, 128 devices: a whole 4x4x4 slice. The times are simulated.
128 devices in a mesh: meta: 8 (over x, z_hi), node: 16 (over y, z_lo, core).
Axes of the slice: x: 4, y: 4, z: 4 (z_hi: 2, z_lo: 2; z = z_hi * 2 + z_lo), core: 2. Of those that a mesh axis runs over, the one named last changes fastest.
Arguments:
- aggregates: bfloat16 [16, 32768, 768], P('meta', 'node'), may hold values from -6 to 6
- batch_ids: int32 [24576], P('node'), may hold values from 0 to 2047
- labels: int32 [24576], P('node'), may hold values from 0 to 152
- w_proj: bfloat16 [16, 768, 512], P('meta'), may hold values from -0.21875 to 0.21875
- w_qk: bfloat16 [512, 128], replicated, may hold values from -0.25 to 0.25
- w_value: bfloat16 [512, 512], replicated, may hold values from -0.25 to 0.25
- w_class: bfloat16 [153, 8192], replicated, may hold values from -0.1875 to 0.1875
Outputs:
- grad_proj: float32 [16, 768, 512], P('meta')
- grad_qk: float32 [512, 128], replicated
- grad_value: float32 [512, 512], replicated
- grad_class: float32 [153, 8192], P(None, 'meta')
- loss: float32 [], replicated
All inputs are finite; a program needn't handle non-finite values.
Results may differ from a plain program's by a relative error of at most 0.024.
Values may be sent and summed in bfloat16 or wider, within the bound.
A program may use at most 128 MiB of HBM per device.

v0:
```python
import jax
import jax.numpy as jnp
from jax import lax
from jax.sharding import PartitionSpec as P


def product(pattern, first_op, second_op):
    return jnp.einsum(pattern, first_op, second_op, preferred_element_type=jnp.float32)


def head_step(hidden, targets, w_qk, w_value, w_class, grad_seed):
    meta_count, node_count, proj_width = hidden.shape
    key_width = w_qk.shape[1] // 2
    key_scale = key_width ** (-0.5)
    query_keys = product("mnp,pc->mnc", hidden, w_qk).astype(jnp.bfloat16)
    queries = query_keys[..., :key_width]
    key_rows = query_keys[..., key_width:]
    values = product("mnp,pe->mne", hidden, w_value).astype(jnp.bfloat16)
    scores = product("inc,jnc->nij", queries, key_rows) * key_scale
    weights = jnp.exp(scores)
    attention = weights / jnp.sum(weights, axis=2, keepdims=True)
    attn_bf = attention.astype(jnp.bfloat16)
    joined_rows = (product("nij,jne->ine", attn_bf, values) + hidden.astype(jnp.float32)).astype(
        jnp.bfloat16
    )
    class_count = w_class.shape[0]
    class_w = w_class.reshape(class_count, meta_count, proj_width)
    logits = product("mnp,cmp->nc", joined_rows, class_w)
    exp_logits = jnp.exp(logits)
    row_total = jnp.sum(exp_logits, axis=1, keepdims=True)
    onehot = (targets[:, None] == jnp.arange(class_count, dtype=jnp.int32)[None, :]).astype(
        jnp.float32
    )
    loss_sum = jnp.sum(jnp.log(row_total[:, 0]) - jnp.sum(onehot * logits, axis=1))
    dlogits = (grad_seed * (exp_logits / row_total - onehot)).astype(jnp.bfloat16)
    grad_class = product("nc,mnp->cmp", dlogits, joined_rows).reshape(
        class_count, meta_count * proj_width
    )
    d_joined = product("nc,cmp->mnp", dlogits, class_w).astype(jnp.bfloat16)
    d_values = product("nij,ine->jne", attn_bf, d_joined).astype(jnp.bfloat16)
    d_attention = product("ine,jne->nij", d_joined, values)
    d_scores = (
        attention
        * (d_attention - jnp.sum(attention * d_attention, axis=2, keepdims=True))
        * key_scale
    ).astype(jnp.bfloat16)
    d_queries = product("nij,jnc->inc", d_scores, key_rows)
    d_keys = product("nij,inc->jnc", d_scores, queries)
    d_query_keys = jnp.concatenate([d_queries, d_keys], axis=2).astype(jnp.bfloat16)
    grad_qk = product("mnp,mnc->pc", hidden, d_query_keys)
    grad_value = product("mnp,mne->pe", hidden, d_values)
    back_rows = (
        d_joined.astype(jnp.float32)
        + product("mnc,pc->mnp", d_query_keys, w_qk)
        + product("mne,pe->mnp", d_values, w_value)
    ).astype(jnp.bfloat16)
    return (loss_sum, grad_qk, grad_value, grad_class, back_rows)


def local(aggregates, batch_ids, labels, w_proj, w_qk, w_value, w_class):
    groups = lax.axis_size("meta")
    batch_total = labels.shape[0] * lax.axis_size("node")
    grad_seed = 1.0 / batch_total**0.5
    gathered = jnp.take(aggregates, batch_ids, axis=1)
    projected = product("pbf,pfd->pbd", gathered, w_proj).astype(jnp.bfloat16)
    joined_in = lax.all_to_all(projected, "meta", split_axis=1, concat_axis=0, tiled=True)
    node_count = joined_in.shape[1]
    own_labels = lax.dynamic_slice_in_dim(labels, lax.axis_index("meta") * node_count, node_count)
    loss_part, grad_qk, grad_value, grad_class, back_rows = head_step(
        joined_in, own_labels, w_qk, w_value, w_class, grad_seed
    )
    returned = lax.all_to_all(back_rows, "meta", split_axis=0, concat_axis=1, tiled=True)
    proj_part = product("pbf,pbd->pfd", gathered, returned)
    col_block = grad_class.shape[1] // groups
    grad_qk, grad_value, class_full, loss_total = lax.psum(
        (grad_qk, grad_value, grad_class, loss_part), ("meta", "node")
    )
    class_own = lax.dynamic_slice_in_dim(
        class_full, lax.axis_index("meta") * col_block, col_block, 1
    )
    grad_proj = lax.psum(proj_part.astype(jnp.bfloat16), "node").astype(jnp.float32)
    return (grad_proj, grad_qk, grad_value, class_own, loss_total / batch_total)


def solution(mesh):
    in_specs = (P("meta", "node", None), P("node"), P("node"), P("meta", None, None), P(), P(), P())
    out_specs = (P("meta", None, None), P(), P(), P(None, "meta"), P())
    return jax.shard_map(local, mesh=mesh, in_specs=in_specs, out_specs=out_specs, check_vma=False)
```

profile of v0, /device:TPU:1, one launch (start us, length us, event | category | flops | bytes accessed | tf_op | source)
XLA Modules:
  0.0 483.6 jit_solution(15714883256654198578)
XLA Ops:
  7.2 0.8 compare_and_fusion
  8.0 0.7 compare_select_fusion
  8.7 20.3 %gather_fusion = bf16[1536,2,768]{2,0,1:T(8,128)(2,1)} fusion(bf16[2,2048,768]{2,1,0:T(8,128)(2,1)} %param.7, s32[2048]{0:T(1024)S(1)} %pad_clamp_fusion), kind=kCustom, calls=%fused_computation | custom fusion | bytes 9443328 | tf_op jit(solution)/shard_map/jit(_take)/gather | solution.py:64
  29.1 5.0 %fusion.6 = bf16[2,1536,512]{2,1,0:T(8,128)(2,1)S(1)} fusion(bf16[2,768,512]{2,1,0:T(8,128)(2,1)S(1)} %copy-done, bf16[1536,2,768]{2,0,1:T(8,128)(2,1)} %gather_fusion, pred[1536]{0:T(1024)(128)(4,1)S(1)} %compare_and_fusion), kind=kOutput, calls=%fused_computation.10 | convolution fusion | flops 2419851264 | bytes 9438720 | tf_op jit(solution)/shard_map/pbf,pfd->pbd/dot_general | solution.py:8
  34.1 14.5 %copy.53 = bf16[2,1536,512]{2,0,1:T(2,128)(2,1)} copy(bf16[2,1536,512]{2,1,0:T(8,128)(2,1)S(1)} %fusion.6) | data formatting | bytes 6291456 | tf_op jit(solution)/shard_map/convert_element_type | solution.py:65
  48.6 8.3 %all-to-all-start = ((bf16[2,1536,512]{2,0,1:T(2,128)(2,1)}), bf16[2,1536,512]{2,0,1:T(2,128)(2,1)}, u32[]{:S(2)}, u32[]{:S(2)}) async-start(bf16[2,1536,512]{2,0,1:T(2,128)(2,1)} %copy.53), calls=%async_computation | async-start | bytes 6291456 | tf_op jit(solution)/shard_map/all_to_all | solution.py:66
  56.9 2.8 copy.78
  59.7 1.6 slice.12
  61.4 0.8 dynamic_slice.6
  62.1 39.5 %all-to-all-done = bf16[2,1536,512]{2,0,1:T(2,128)(2,1)} async-done(((bf16[2,1536,512]{2,0,1:T(2,128)(2,1)}), bf16[2,1536,512]{2,0,1:T(2,128)(2,1)}, u32[]{:S(2)}, u32[]{:S(2)}) %all-to-all-start) | async-done | bytes 3145760 | tf_op jit(solution)/shard_map/all_to_all | solution.py:66
  101.6 2.6 copy.54
  104.2 1.0 convolution_convert_fusion.3
  105.2 0.3 fusion.71
  105.5 0.3 copy-done.2
  105.8 3.5 convolution_convert_fusion
  109.3 1.2 fusion.47
  110.5 4.1 fusion.18
  114.6 4.0 fusion.1
  118.6 2.9 select_reduce_fusion
  121.6 3.3 convert_bitcast_fusion.1
  124.9 1.6 copy-done.6
  126.6 4.6 fusion.15
  131.2 3.7 fusion.37
  134.9 2.8 fusion.38
  137.7 4.4 convert_bitcast_fusion
  142.1 5.4 %fusion.34 = f32[512,512]{1,0:T(8,128)} fusion(bf16[16,192,512]{2,1,0:T(8,128)(2,1)S(1)} %bitcast.67, bf16[16,192,512]{2,0,1:T(8,128)(2,1)S(1)} %convert_bitcast_fusion), kind=kOutput, calls=%fused_computation.37 | convolution fusion | flops 1610612736 | bytes 7340032 | tf_op jit(solution)/shard_map/mnp,mne->pe/dot_general | solution.py:8
  147.5 3.9 fusion.11
  151.4 0.4 pad_maximum_fusion
  151.9 2.9 add_convert_fusion
  154.7 4.5 all-to-all-start.1
  159.2 0.2 all-reduce.6.cloned.1.call-start
  159.4 2.7 fusion.62
  162.2 2.9 copy.74
  165.1 1.1 pad.3
  166.1 6.7 %copy.79 = f32[20,8,16,512]{3,1,2,0:T(8,128)} copy(f32[20,8,16,512]{3,2,1,0:T(8,128)S(1)} %bitcast.70) | data formatting | bytes 10485760
  172.8 1.7 convolution_bitcast_fusion
  174.5 0.3 all-reduce.4.cloned.1.call-start
  174.8 32.4 %all-to-all-done.1 = bf16[16,192,512]{2,1,0:T(8,128)(2,1)} async-done(((bf16[16,192,512]{2,1,0:T(8,128)(2,1)}), bf16[16,192,512]{2,1,0:T(8,128)(2,1)}, u32[]{:S(2)}, u32[]{:S(2)}) %all-to-all-start.1) | async-done | bytes 3145760 | tf_op jit(solution)/shard_map/all_to_all | solution.py:72
  207.2 2.2 copy.70
  209.3 6.4 %fusion.28 = bf16[2,768,512]{2,1,0:T(8,128)(2,1)} fusion(bf16[2,1536,512]{2,1,0:T(8,128)(2,1)S(1)} %bitcast.72, bf16[1536,2,768]{2,0,1:T(8,128)(2,1)} %gather_fusion, pred[1536]{0:T(1024)(128)(4,1)S(1)} %compare_and_fusion), kind=kOutput, calls=%fused_computation.29 | convolution fusion | flops 2419064832 | bytes 9438720 | tf_op jit(solution)/shard_map/pbf,pbd->pfd/dot_general | solution.py:8
  215.7 0.6 subtract_reduce_fusion
  216.3 66.0 %psum.39 = f32[]{:T(128)} all-reduce(f32[]{:T(128)} %subtract_reduce_fusion), channel_id=1, replica_groups=mesh['meta'=8,'node'=16] {'meta','node'}, use_global_device_ids=true, to_apply=%region_9.10 | all-reduce | flops 1 | bytes 8 | tf_op jit(solution)/shard_map/psum | solution.py:75
  283.0 64.4 %all-reduce.6.cloned.1.call-done = (f32[512,128]{1,0:T(8,128)}, f32[512,512]{1,0:T(8,128)}, f32[153,8192]{1,0:T(8,128)}) async-done(((f32[512,128]{1,0:T(8,128)}, f32[512,512]{1,0:T(8,128)}, f32[153,8192]{1,0:T(8,128)}), (f32[512,128]{1,0:T(8,128)}, f32[512,512]{1,0:T(8,128)}, f32[153,8192]{1,0:T(8,128)})) %all-reduce.6.cloned.1.call-update) | async-done | bytes 6324240 | tf_op jit(solution)/shard_map/psum | solution.py:75
  347.4 2.1 constant_dynamic-slice_fusion
  349.6 120.7 %all-reduce.4.cloned.1.call-done = bf16[2,768,512]{2,1,0:T(8,128)(2,1)} async-done(((bf16[2,768,512]{2,1,0:T(8,128)(2,1)}), bf16[2,768,512]{2,1,0:T(8,128)(2,1)}) %all-reduce.4.cloned.1.call-update) | async-done | bytes 1572880 | tf_op jit(solution)/shard_map/psum | solution.py:81
  470.3 3.5 convert_element_type.68
  473.8 0.7 copy.127
  474.5 1.0 copy.128
  (35 shorter events, 0.1 us)
Async XLA Ops:
  7.2 21.9 %copy-start = (bf16[2,768,512]{2,1,0:T(8,128)(2,1)S(1)}, bf16[2,768,512]{2,1,0:T(8,128)(2,1)}, u32[]{:S(2)}) copy-start(bf16[2,768,512]{2,1,0:T(8,128)(2,1)} %param.10) | copy-start | bytes 4718596
  48.6 53.1 %all-to-all-start = ((bf16[2,1536,512]{2,0,1:T(2,128)(2,1)}), bf16[2,1536,512]{2,0,1:T(2,128)(2,1)}, u32[]{:S(2)}, u32[]{:S(2)}) async-start(bf16[2,1536,512]{2,0,1:T(2,128)(2,1)} %copy.53), calls=%async_computation | async-start | bytes 6291456 | tf_op jit(solution)/shard_map/all_to_all | solution.py:66
  101.6 2.6 copy-start.13
  104.2 1.7 copy-start.2
  104.2 1.6 copy-start.14
  110.5 4.1 copy-start.3
  114.6 4.0 copy-start.9
  118.6 2.9 copy-start.8
  121.6 5.0 %copy-start.10 = (bf16[16,192,512]{2,1,0:T(8,128)(2,1)S(1)}, bf16[16,192,512]{2,1,0:T(8,128)(2,1)}, u32[]{:S(2)}) copy-start(bf16[16,192,512]{2,1,0:T(8,128)(2,1)} %convolution_convert_fusion) | copy-start | bytes 9437188
  124.9 1.6 copy-start.6
  137.7 4.4 copy-start.4
  142.1 5.4 %copy-start.15 = (bf16[512,512]{1,0:T(8,128)(2,1)S(1)}, bf16[512,512]{1,0:T(8,128)(2,1)}, u32[]{:S(2)}) copy-start(bf16[512,512]{1,0:T(8,128)(2,1)} %param.12) | copy-start | bytes 1572868
  147.5 3.9 copy-start.12
  147.5 4.3 copy-start.7
  154.7 52.5 %all-to-all-start.1 = ((bf16[16,192,512]{2,1,0:T(8,128)(2,1)}), bf16[16,192,512]{2,1,0:T(8,128)(2,1)}, u32[]{:S(2)}, u32[]{:S(2)}) async-start(bf16[16,192,512]{2,1,0:T(8,128)(2,1)} %add_convert_fusion), calls=%async_computation.1 | async-start | bytes 6291456 | tf_op jit(solution)/shard_map/all_to_all | solution.py:72
  159.2 188.2 %all-reduce.6.cloned.1.call-start = ((), (), s32[]{:S(2)}) async-start(), calls=%async_computation.3 | async-start | bytes 13107200 | tf_op jit(solution)/shard_map/psum | solution.py:75
  166.1 6.7 %copy-start.5 = (bf16[2,8,192,512]{3,2,0,1:T(8,128)(2,1)S(1)}, bf16[2,8,192,512]{3,2,0,1:T(8,128)(2,1)}, u32[]{:S(2)}) copy-start(bf16[2,8,192,512]{3,2,0,1:T(8,128)(2,1)} %copy-done.2) | copy-start | bytes 9437188
  174.5 295.7 %all-reduce.4.cloned.1.call-start = ((), (), s32[]{:S(2)}) async-start(), calls=%async_computation.2 | async-start | bytes 3145728 | tf_op jit(solution)/shard_map/psum | solution.py:81
  347.4 126.3 %copy-start.16 = (f32[512,128]{1,0:T(8,128)S(1)}, f32[512,128]{1,0:T(8,128)}, u32[]{:S(2)}) copy-start(f32[512,128]{1,0:T(8,128)} %get-tuple-element.14) | copy-start | bytes 786436
  347.4 127.0 %copy-start.11 = (f32[512,512]{1,0:T(8,128)S(1)}, f32[512,512]{1,0:T(8,128)}, u32[]{:S(2)}) copy-start(f32[512,512]{1,0:T(8,128)} %get-tuple-element.15) | copy-start | bytes 3145732
  347.4 128.0 %copy-start.1 = (bf16[2,768,512]{2,1,0:T(8,128)(2,1)S(1)}, bf16[2,768,512]{2,1,0:T(8,128)(2,1)}, u32[]{:S(2)}) copy-start(bf16[2,768,512]{2,1,0:T(8,128)(2,1)} %param.10) | copy-start | bytes 4718596
Sparse Core Ops, SparseCore 0:
  174.7 172.7 all-reduce.5
  350.5 119.7 all-reduce.3
where the time goes:
time: 490 us; the launch traced here: 484 us
  waiting for transfers between devices  257 us (52%)
  blocking collectives  66 us (13%)
  local copies, waits for them, and re-layouts  61.5 us (13%)
  matrix products  59.4 us (12%)
  between operations  16.3 us (3%)
  starting transfers between devices  13.2 us (3%)
  other arithmetic  10.1 us (2%)
    psum x1, waiting for transfers between devices, local(): lax.psum(proj_part.astype(jnp.bfloat16), 'node').astype(jnp.float32)  121 us
    psum x1, blocking collectives, local(): lax.psum((grad_qk, grad_value, grad_class, loss_part), ('meta', 'node'))  66 us
    psum x1, waiting for transfers between devices, local(): lax.psum((grad_qk, grad_value, grad_class, loss_part), ('meta', 'node'))  64.4 us
    dot_general x16, matrix products, product(): jnp.einsum(pattern, first_op, second_op, preferred_element_type=jnp.float32)  58.2 us
    all_to_all x1, waiting for transfers between devices, local(): lax.all_to_all(projected, 'meta', split_axis=1, concat_axis=0, tiled=True)  39.5 us
    all_to_all x1, waiting for transfers between devices, local(): lax.all_to_all(back_rows, 'meta', split_axis=0, concat_axis=1, tiled=True)  32.4 us
    gather x1, local copies, waits for them, and re-layouts, local(): gathered = jnp.take(aggregates, batch_ids, axis=1)  20.3 us
    convert_element_type x1, local copies, waits for them, and re-layouts, local(): projected = product('pbf,pfd->pbd', gathered, w_proj).astype(jnp.bfloat16)  14.5 us
  transfers between devices with their start and end apart: 4, of which 4 were waited for; matrix products, arithmetic and copies ran while one was open for 7% of the time, Pallas kernels for 0%

commit v1 on v0

v1 whole, which is shorter than its diff:
```python
import functools

import jax
import jax.numpy as jnp
from jax import lax
from jax.experimental import pallas as pl
from jax.experimental.pallas import tpu as pltpu
from jax.sharding import PartitionSpec as P

MESH = pl.DeviceIdType.MESH
F32 = jnp.float32
BF16 = jnp.bfloat16
GROUPS = 8
CHIPS = 8
PAPERS = 192
BLOCK = 16
CLASS_PAD = 160


def dot(a, b):
    return jnp.dot(a, b, preferred_element_type=F32)


def dot_nt(a, b):
    return lax.dot_general(a, b, (((1,), (1,)), ((), ())), preferred_element_type=F32)


def dot_tn(a, b):
    return lax.dot_general(a, b, (((0,), (0,)), ((), ())), preferred_element_type=F32)


def remote(src, dst, send_sem, recv_sem, where):
    return pltpu.make_async_remote_copy(
        src_ref=src, dst_ref=dst, send_sem=send_sem, recv_sem=recv_sem, device_id=where, device_id_type=MESH
    )


def front_kernel(ids_ref, agg_ref, w_ref, gathered_ref, hidden_ref, outbox, send_sem, recv_sem, own_sem):
    me = lax.axis_index("meta")
    barrier = pltpu.get_barrier_semaphore()
    for j in range(1, GROUPS):
        pl.semaphore_signal(barrier, inc=1, device_id={"meta": lax.rem(me + j, GROUPS)}, device_id_type=MESH)
    pl.semaphore_wait(barrier, GROUPS - 1)

    rows = agg_ref.shape[1]

    def work(peer):
        at = pl.ds(pl.multiple_of(peer * PAPERS, PAPERS), PAPERS)
        picks = ids_ref[at, :] == lax.broadcasted_iota(jnp.int32, (PAPERS, rows), 1)
        picks = picks.astype(F32).astype(BF16)
        for m in range(2):
            got = dot(picks, agg_ref[m]).astype(BF16)
            gathered_ref[m, at, :] = got
            outbox[peer, m] = dot(got, w_ref[m]).astype(BF16)

    def copy_to(peer):
        return remote(
            outbox.at[peer], hidden_ref.at[pl.ds(2 * me, 2)], send_sem.at[peer], recv_sem.at[me], {"meta": peer}
        )

    def step(j, carry):
        peer = lax.rem(me + j, GROUPS)
        work(peer)
        copy_to(peer).start()
        return carry

    lax.fori_loop(1, GROUPS, step, 0)
    work(me)
    own = pltpu.make_async_copy(outbox.at[me], hidden_ref.at[pl.ds(2 * me, 2)], own_sem)
    own.start()
    for j in range(1, GROUPS):
        peer = lax.rem(me + j, GROUPS)
        remote(
            outbox.at[peer], hidden_ref.at[pl.ds(2 * peer, 2)], send_sem.at[peer], recv_sem.at[peer], {"meta": peer}
        ).wait()
    own.wait()


def front(ids, aggregates, w_proj):
    count, rows, feat = aggregates.shape
    width = w_proj.shape[2]
    batch = ids.shape[0]
    vmem = pl.BlockSpec(memory_space=pltpu.VMEM)
    return pl.pallas_call(
        front_kernel,
        out_shape=(
            jax.ShapeDtypeStruct((count, batch, feat), BF16),
            jax.ShapeDtypeStruct((GROUPS * count, PAPERS, width), BF16),
        ),
        in_specs=[vmem] * 3,
        out_specs=(vmem, pl.BlockSpec(memory_space=pl.ANY)),
        scratch_shapes=[
            pltpu.VMEM((GROUPS, count, PAPERS, width), BF16),
            pltpu.SemaphoreType.DMA((GROUPS,)),
            pltpu.SemaphoreType.DMA((GROUPS,)),
            pltpu.SemaphoreType.DMA,
        ],
        compiler_params=pltpu.CompilerParams(
            collective_id=0, has_side_effects=True, vmem_limit_bytes=56 * 1024 * 1024
        ),
    )(ids, aggregates, w_proj)


def back_kernel(
    seed, class_count,
    hidden, w_class, w_all, labels, gathered,
    proj_out, qk_out, value_out, class_out, loss_out,
    joined, d_joined, values, attention, kq, d_vq, returned,
    cls, cls_in, cls_chip, cls_g, cls_meta, cls_all,
    qv_acc, qv, qv_in, qv_chip, qv_meta, qv_all,
    gp, gp_in, gp_chip, gp_all, loss_meta, loss_node,
    send_sem, recv_sem, sib_send, sib_recv,
):
    me = lax.axis_index("meta")
    node = lax.axis_index("node")
    chip, core = node // 2, lax.rem(node, 2)
    other = 1 - core
    sibling = {"node": 2 * chip + other}
    groups = [lax.rem(me + j, GROUPS) for j in range(1, GROUPS)]
    chips = [lax.rem(chip + j, CHIPS) for j in range(1, CHIPS)]

    barrier = pltpu.get_barrier_semaphore()
    for g in groups:
        pl.semaphore_signal(barrier, inc=1, device_id={"meta": g}, device_id_type=MESH)
    for k in chips:
        pl.semaphore_signal(barrier, inc=1, device_id={"node": 2 * k + core}, device_id_type=MESH)
    pl.semaphore_signal(barrier, inc=1, device_id=sibling, device_id_type=MESH)
    pl.semaphore_wait(barrier, GROUPS - 1 + CHIPS)

    def to_group(phase, g, src, dst):
        return remote(src, dst, send_sem.at[phase, g], recv_sem.at[phase, me], {"meta": g})

    def from_group(phase, g, dst):
        return remote(dst, dst, send_sem.at[phase, g], recv_sem.at[phase, g], {"meta": g})

    def to_chip(phase, k, src, dst):
        return remote(src, dst, send_sem.at[phase, k], recv_sem.at[phase, chip], {"node": 2 * k + core})

    def from_chip(phase, k, dst):
        return remote(dst, dst, send_sem.at[phase, k], recv_sem.at[phase, k], {"node": 2 * k + core})

    def to_sibling(phase, src, dst):
        return remote(src, dst, sib_send.at[phase], sib_recv.at[phase], sibling)

    meta_count, papers, width = hidden.shape
    pad = w_class.shape[0]
    key = 64
    scale = key ** (-0.5)
    side = BLOCK * meta_count
    row_paper = lax.rem(lax.broadcasted_iota(jnp.int32, (side, side), 0), BLOCK)
    col_paper = lax.rem(lax.broadcasted_iota(jnp.int32, (side, side), 1), BLOCK)
    same = row_paper == col_paper
    lane = lax.broadcasted_iota(jnp.int32, (side, 2 * key), 1)
    first = lane < key

    def forward(b, carry):
        at = pl.ds(pl.multiple_of(b * BLOCK, BLOCK), BLOCK)
        h = hidden[:, at, :].reshape(side, width)
        mixed = dot(h, w_all[...]).astype(BF16)
        v = mixed[:, :width]
        qk = mixed[:, width : width + 2 * key]
        swapped = mixed[:, width + 2 * key :]
        values[b] = v
        kq[b] = swapped
        q = jnp.where(first, qk.astype(F32), 0.0).astype(BF16)
        scores = dot_nt(q, swapped) * scale
        weights = jnp.where(same, jnp.exp(scores), 0.0)
        att = weights / jnp.sum(weights, axis=1, keepdims=True)
        attention[b] = att
        out = (dot(att.astype(BF16), v) + h.astype(F32)).astype(BF16)
        joined[:, at, :] = out.reshape(meta_count, BLOCK, width)
        return carry

    lax.fori_loop(0, papers // BLOCK, forward, 0)

    def columns(m):
        return pl.ds(pl.multiple_of(m * width, width), width)

    logits = lax.fori_loop(
        0, meta_count, lambda m, t: t + dot_nt(joined[m], w_class[:, columns(m)]), jnp.zeros((papers, pad), F32)
    )
    class_at = lax.broadcasted_iota(jnp.int32, (papers, pad), 1)
    exps = jnp.where(class_at < class_count, jnp.exp(logits), 0.0)
    total = jnp.sum(exps, axis=1, keepdims=True)
    own = pl.ds(pl.multiple_of(me * papers, papers), papers)
    onehot = (labels[own, :] == class_at).astype(F32)
    loss_rows = jnp.log(total) - jnp.sum(onehot * logits, axis=1, keepdims=True)
    loss_meta[me] = jnp.zeros((8, 128), F32) + jnp.sum(loss_rows)
    dlogits = (seed * (exps / total - onehot)).astype(BF16)

    def classes(g, carry):
        for half in range(2):
            m = 2 * g + half
            d_joined[m] = dot(dlogits, w_class[:, columns(m)]).astype(BF16)
            grad = dot_tn(dlogits, joined[m]).astype(BF16)
            for q in range(4):
                for part in range(2):
                    cls[part, 4 * half + q, g] = grad[
                        part * (pad // 2) : (part + 1) * (pad // 2), q * 128 : (q + 1) * 128
                    ]
        return carry

    lax.fori_loop(0, GROUPS, classes, 0)
    c0 = to_sibling(0, cls.at[other], cls_in)
    c0.start()

    def backward(b, carry):
        at = pl.ds(pl.multiple_of(b * BLOCK, BLOCK), BLOCK)
        dj = d_joined[:, at, :].reshape(side, width)
        att = attention[b]
        d_val = dot_tn(att.astype(BF16), dj)
        d_att = dot_nt(dj, values[b])
        mean = jnp.sum(att * d_att, axis=1, keepdims=True)
        d_scores = (att * (d_att - mean) * scale).astype(BF16)
        swapped = kq[b]
        d_qk = jnp.where(first, dot(d_scores, swapped), dot_tn(d_scores, swapped))
        d_vq[:, at, :width] = d_val.astype(BF16).reshape(meta_count, BLOCK, width)
        d_vq[:, at, width:] = d_qk.astype(BF16).reshape(meta_count, BLOCK, 2 * key)
        return carry

    lax.fori_loop(0, papers // BLOCK, backward, 0)

    qv_acc[...] = jnp.zeros_like(qv_acc)
    mixed_width = width + 2 * key
    back = joined

    def returns(j, carry):
        g = lax.rem(me + j, GROUPS)
        for half in range(2):
            m = 2 * g + half
            rows = d_vq[m]
            back[m] = (d_joined[m].astype(F32) + dot_nt(rows, w_all[:, :mixed_width])).astype(BF16)
            qv_acc[...] += dot_tn(hidden[m], rows)
        return carry

    def slot(g):
        return returned.at[:, pl.ds(pl.multiple_of(g * papers, papers), papers), :]

    def send_back(j, carry):
        returns(j, carry)
        g = lax.rem(me + j, GROUPS)
        to_group(0, g, back.at[pl.ds(2 * g, 2)], slot(me)).start()
        return carry

    lax.fori_loop(1, GROUPS, send_back, 0)
    returns(0, 0)
    for half in range(2):
        returned[half, pl.ds(pl.multiple_of(me * papers, papers), papers), :] = back[2 * me + half]

    part_rows = qv.shape[2]
    for part in range(2):
        for k in range(CHIPS):
            start = (part * CHIPS + k) * part_rows
            qv[part, k] = qv_acc[start : start + part_rows, :].astype(BF16)
    q0 = to_sibling(1, qv.at[other], qv_in)
    q0.start()

    c0.wait_recv()
    q0.wait_recv()

    def pair_sum(k, carry):
        cls_in[k] = (cls[core, k].astype(F32) + cls_in[k].astype(F32)).astype(BF16)
        qv_in[k] = (qv[core, k].astype(F32) + qv_in[k].astype(F32)).astype(BF16)
        return carry

    lax.fori_loop(0, CHIPS, pair_sum, 0)
    for k in chips:
        to_chip(1, k, cls_in.at[k], cls_chip.at[chip]).start()
        to_chip(2, k, qv_in.at[k], qv_chip.at[chip]).start()
    cls_chip[chip] = cls_in[chip]
    qv_chip[chip] = qv_in[chip]
    for k in chips:
        from_chip(1, k, cls_chip.at[k]).wait_recv()
        from_chip(2, k, qv_chip.at[k]).wait_recv()

    def chip_sum(g, carry):
        cls_g[g] = jnp.sum(cls_chip[:, g].astype(F32), axis=0).astype(BF16)
        return carry

    lax.fori_loop(0, GROUPS, chip_sum, 0)
    qv_meta[me] = jnp.sum(qv_chip[...].astype(F32), axis=0).astype(BF16)
    cls_meta[me] = cls_g[me]
    for g in groups:
        to_group(3, g, cls_g.at[g], cls_meta.at[me]).start()
        to_group(4, g, qv_meta.at[me], qv_meta.at[me]).start()
        to_group(5, g, loss_meta.at[me], loss_meta.at[me]).start()

    for g in groups:
        from_group(0, g, slot(g)).wait_recv()

    part_feat = gp.shape[2]

    def project(m):
        grad = dot_tn(gathered[m], returned[m])
        for k in range(CHIPS):
            gp[m, k] = grad[k * part_feat : (k + 1) * part_feat].astype(BF16)

    project(other)
    g0 = to_sibling(2, gp.at[other], gp_in)
    g0.start()
    project(core)

    for g in groups:
        from_group(3, g, cls_meta.at[g]).wait_recv()
        from_group(4, g, qv_meta.at[g]).wait_recv()
        from_group(5, g, loss_meta.at[g]).wait_recv()
    cls_all[core, chip] = jnp.sum(cls_meta[...].astype(F32), axis=0).astype(BF16)
    qv_all[core, chip] = jnp.sum(qv_meta[...].astype(F32), axis=0).astype(BF16)
    loss_node[core, chip] = jnp.sum(loss_meta[...], axis=0)
    for k in chips:
        to_chip(6, k, cls_all.at[core, chip], cls_all.at[core, chip]).start()
        to_chip(7, k, qv_all.at[core, chip], qv_all.at[core, chip]).start()
        to_chip(8, k, loss_node.at[core, chip], loss_node.at[core, chip]).start()

    g0.wait_recv()

    def pair_proj(k, carry):
        gp_in[k] = (gp[core, k].astype(F32) + gp_in[k].astype(F32)).astype(BF16)
        return carry

    lax.fori_loop(0, CHIPS, pair_proj, 0)
    for k in chips:
        to_chip(9, k, gp_in.at[k], gp_chip.at[chip]).start()
    gp_chip[chip] = gp_in[chip]

    for k in chips:
        from_chip(6, k, cls_all.at[core, k]).wait_recv()
        from_chip(7, k, qv_all.at[core, k]).wait_recv()
        from_chip(8, k, loss_node.at[core, k]).wait_recv()
    last = [
        to_sibling(3, cls_all.at[core], cls_all.at[core]),
        to_sibling(4, qv_all.at[core], qv_all.at[core]),
        to_sibling(5, loss_node.at[core], loss_node.at[core]),
    ]
    for copy in last:
        copy.start()

    for k in chips:
        from_chip(9, k, gp_chip.at[k]).wait_recv()
    gp_all[core, chip] = jnp.sum(gp_chip[...].astype(F32), axis=0).astype(BF16)
    for k in chips:
        to_chip(10, k, gp_all.at[core, chip], gp_all.at[core, chip]).start()

    def across(k):
        return remote(
            gp_all.at[core, k], gp_all.at[core, k], send_sem.at[11, k], recv_sem.at[11, k], sibling
        )

    def across_in(k):
        return remote(
            gp_all.at[other, k], gp_all.at[other, k], send_sem.at[11, k], recv_sem.at[11, k], sibling
        )

    across(chip).start()

    remote(cls_all.at[other], cls_all.at[other], sib_send.at[3], sib_recv.at[3], sibling).wait_recv()
    remote(qv_all.at[other], qv_all.at[other], sib_send.at[4], sib_recv.at[4], sibling).wait_recv()
    remote(loss_node.at[other], loss_node.at[other], sib_send.at[5], sib_recv.at[5], sibling).wait_recv()
    half_rows = pad // 2
    for k in range(CHIPS):
        lanes = slice(k * 128, (k + 1) * 128)
        class_out[:half_rows, lanes] = cls_all[0, k].astype(F32)
        class_out[half_rows:, lanes] = cls_all[1, k][: class_count - half_rows].astype(F32)
        for part in range(2):
            start = (part * CHIPS + k) * part_rows
            block = qv_all[part, k].astype(F32)
            value_out[start : start + part_rows, :] = block[:, :width]
            qk_out[start : start + part_rows, :] = block[:, width:]
    loss_out[...] = jnp.sum(loss_node[...].reshape(2 * CHIPS, 8, 128), axis=0)

    for k in chips:
        from_chip(10, k, gp_all.at[core, k]).wait_recv()
        across(k).start()

    def emit(part, k):
        at = pl.ds(pl.multiple_of(k * part_feat, part_feat), part_feat)
        proj_out[part, at, :] = gp_all[part, k].astype(F32)

    for k in [chip] + chips:
        emit(core, k)
    for k in [chip] + chips:
        across_in(k).wait_recv()
        emit(other, k)

    c0.wait_send()
    q0.wait_send()
    g0.wait_send()
    for copy in last:
        copy.wait_send()
    for g in groups:
        to_group(0, g, back.at[pl.ds(2 * g, 2)], slot(me)).wait_send()
        to_group(3, g, cls_g.at[g], cls_meta.at[me]).wait_send()
        to_group(4, g, qv_meta.at[me], qv_meta.at[me]).wait_send()
        to_group(5, g, loss_meta.at[me], loss_meta.at[me]).wait_send()
    for k in chips:
        to_chip(1, k, cls_in.at[k], cls_chip.at[chip]).wait_send()
        to_chip(2, k, qv_in.at[k], qv_chip.at[chip]).wait_send()
        to_chip(6, k, cls_all.at[core, chip], cls_all.at[core, chip]).wait_send()
        to_chip(7, k, qv_all.at[core, chip], qv_all.at[core, chip]).wait_send()
        to_chip(8, k, loss_node.at[core, chip], loss_node.at[core, chip]).wait_send()
        to_chip(9, k, gp_in.at[k], gp_chip.at[chip]).wait_send()
        to_chip(10, k, gp_all.at[core, chip], gp_all.at[core, chip]).wait_send()
    for k in [chip] + chips:
        across(k).wait_send()


def back_step(hidden, w_class, w_all, labels, gathered, class_count, seed):
    metas, papers, width = hidden.shape
    feat = gathered.shape[2]
    batch = gathered.shape[1]
    side = BLOCK * metas
    blocks = papers // BLOCK
    mixed = width + 128
    half = CLASS_PAD // 2
    vmem = pl.BlockSpec(memory_space=pltpu.VMEM)
    part = feat // CHIPS
    rows = width // (2 * CHIPS)
    return pl.pallas_call(
        functools.partial(back_kernel, seed, class_count),
        out_shape=(
            jax.ShapeDtypeStruct((2, feat, width), F32),
            jax.ShapeDtypeStruct((width, 128), F32),
            jax.ShapeDtypeStruct((width, width), F32),
            jax.ShapeDtypeStruct((class_count, 2 * width), F32),
            jax.ShapeDtypeStruct((8, 128), F32),
        ),
        in_specs=[vmem] * 5,
        out_specs=(vmem,) * 5,
        scratch_shapes=[
            pltpu.VMEM((metas, papers, width), BF16),
            pltpu.VMEM((metas, papers, width), BF16),
            pltpu.VMEM((blocks, side, width), BF16),
            pltpu.VMEM((blocks, side, side), F32),
            pltpu.VMEM((blocks, side, 128), BF16),
            pltpu.VMEM((metas, papers, mixed), BF16),
            pltpu.VMEM((2, batch, width), BF16),
            pltpu.VMEM((2, CHIPS, GROUPS, half, 128), BF16),
            pltpu.VMEM((CHIPS, GROUPS, half, 128), BF16),
            pltpu.VMEM((CHIPS, GROUPS, half, 128), BF16),
            pltpu.VMEM((GROUPS, half, 128), BF16),
            pltpu.VMEM((GROUPS, half, 128), BF16),
            pltpu.VMEM((2, CHIPS, half, 128), BF16),
            pltpu.VMEM((width, mixed), F32),
            pltpu.VMEM((2, CHIPS, rows, mixed), BF16),
            pltpu.VMEM((CHIPS, rows, mixed), BF16),
            pltpu.VMEM((CHIPS, rows, mixed), BF16),
            pltpu.VMEM((GROUPS, rows, mixed), BF16),
            pltpu.VMEM((2, CHIPS, rows, mixed), BF16),
            pltpu.VMEM((2, CHIPS, part, width), BF16),
            pltpu.VMEM((CHIPS, part, width), BF16),
            pltpu.VMEM((CHIPS, part, width), BF16),
            pltpu.VMEM((2, CHIPS, part, width), BF16),
            pltpu.VMEM((GROUPS, 8, 128), F32),
            pltpu.VMEM((2, CHIPS, 8, 128), F32),
            pltpu.SemaphoreType.DMA((12, 8)),
            pltpu.SemaphoreType.DMA((12, 8)),
            pltpu.SemaphoreType.DMA((6,)),
            pltpu.SemaphoreType.DMA((6,)),
        ],
        compiler_params=pltpu.CompilerParams(
            collective_id=1, has_side_effects=True, vmem_limit_bytes=60 * 1024 * 1024
        ),
    )(hidden, w_class, w_all, labels, gathered)


def local(aggregates, batch_ids, labels, w_proj, w_qk, w_value, w_class):
    batch_total = labels.shape[0] * lax.axis_size("node")
    class_count = w_class.shape[0]
    key = w_qk.shape[1] // 2
    gathered, hidden = front(batch_ids[:, None], aggregates, w_proj)
    w_all = jnp.concatenate([w_value, w_qk, w_qk[:, key:], w_qk[:, :key]], axis=1)
    w_pad = jnp.pad(w_class, ((0, CLASS_PAD - class_count), (0, 0)))
    grad_proj, grad_qk, grad_value, grad_class, loss = back_step(
        hidden, w_pad, w_all, labels[:, None], gathered, class_count, 1.0 / batch_total**0.5
    )
    return (grad_proj, grad_qk, grad_value, grad_class, loss[0, 0] / batch_total)


def solution(mesh):
    in_specs = (P("meta", "node", None), P("node"), P("node"), P("meta", None, None), P(), P(), P())
    out_specs = (P("meta", None, None), P(), P(), P(None, "meta"), P())
    return jax.shard_map(local, mesh=mesh, in_specs=in_specs, out_specs=out_specs, check_vma=False)
```

time: 490 us -> 216 us (0.44)
  waiting for transfers between devices: 257 us -> 0 us
  Pallas kernels: 0 us -> 195 us
  blocking collectives: 66 us -> 0 us
  matrix products: 59.4 us -> 0 us
  local copies, waits for them, and re-layouts: 61.5 us -> 12.8 us
  between operations: 16.3 us -> 2.49 us
  starting transfers between devices: 13.2 us -> 0 us
  other arithmetic: 10.1 us -> 2.27 us
    pallas_call x0 -> x2, Pallas kernels: none -> 195 us  [the longest x1 138 us: back_step(): pl.pallas_call(functools.partial(back_kernel, seed, class_count), out_sha...]
    psum x2 -> x0, waiting for transfers between devices: 185 us -> none  [the longest x1 121 us: local(): lax.psum(proj_part.astype(jnp.bfloat16), 'node').astype(jnp.float32)]
    all_to_all x2 -> x0, waiting for transfers between devices: 71.9 us -> none  [the longest x1 39.5 us: local(): lax.all_to_all(projected, 'meta', split_axis=1, concat_axis=0, tiled=True)]
    psum x1 -> x0, blocking collectives: 66 us -> none  [local(): lax.psum((grad_qk, grad_value, grad_class, loss_part), ('meta', 'node'))]
    dot_general x16 -> x0, matrix products: 58.2 us -> none  [product(): jnp.einsum(pattern, first_op, second_op, preferred_element_type=jnp.float32)]
    gather x1 -> x0, local copies, waits for them, and re-layouts: 20.3 us -> none  [local(): gathered = jnp.take(aggregates, batch_ids, axis=1)]
    convert_element_type x1 -> x0, local copies, waits for them, and re-layouts: 14.5 us -> none  [local(): projected = product('pbf,pfd->pbd', gathered, w_proj).astype(jnp.bfloat16)]
    all_to_all x2 -> x0, starting transfers between devices: 12.8 us -> none  [the longest x1 8.31 us: local(): lax.all_to_all(projected, 'meta', split_axis=1, concat_axis=0, tiled=True)]
  transfers between devices with their start and end apart: 4 -> 0, of which waited for: 4 -> 0; matrix products, arithmetic and copies ran while one was open for 7% -> 0% of each run, Pallas kernels for 0% -> 0%
where the time goes in v1:
time: 216 us; the launch traced here: 212 us
  Pallas kernels  195 us (90%)
  local copies, waits for them, and re-layouts  12.8 us (6%)
  between operations  2.49 us (1%)
  other arithmetic  2.27 us (1%)
    pallas_call x1, Pallas kernels, back_step(): pl.pallas_call(functools.partial(back_kernel, seed, class_count), out_sha...  138 us
    pallas_call x1, Pallas kernels, front(): pl.pallas_call(front_kernel, out_shape=(jax.ShapeDtypeStruct((count, batc...  56.4 us
    unnamed x16, local copies, waits for them, and re-layouts  6.5 us

profile of v1, /device:TPU:1, one launch (start us, length us, event | category | flops | bytes accessed | tf_op | source)
XLA Modules:
  0.0 212.2 jit_solution(17093532345332839826)
XLA Ops:
  0.6 0.0 copy-start.5
  0.6 0.0 copy-start.4
  0.7 1.1 fusion
  1.7 0.0 copy-start
  1.8 2.3 %pad_maximum_fusion.w_all = bf16[512,768]{1,0:T(8,128)(2,1)} fusion(bf16[512,64]{1,0:T(8,128)(2,1)S(1)} %get-tuple-element.20, bf16[512,64]{1,0:T(8,128)(2,1)S(1)} %get-tuple-element.19, bf16[512,128]{1,0:T(8,128)(2,1)} %param.11, bf16[512,512]{1,0:T(8,128)(2,1)} %param.12), kind=kLoop, calls=%fused_computation | loop fusion | flops 3145728 | bytes 1572864 | tf_op jit(solution)/shard_map/concatenate | solution.py:471
  4.0 0.0 copy-done.4
  4.0 1.1 broadcast_in_dim.8.ids_ref
  5.2 0.0 copy-done.5
  5.2 1.2 broadcast_in_dim.9.labels
  6.4 0.0 copy-done
  6.4 1.7 pad.4.w_class
  8.1 56.4 %shard_map.110 = (bf16[2,1536,768]{2,1,0:T(8,128)(2,1)}, bf16[16,192,512]{2,1,0:T(8,128)(2,1)}) custom-call(s32[1536,1]{1,0:T(8,128)} %broadcast_in_dim.8.ids_ref, bf16[2,2048,768]{2,1,0:T(8,128)(2,1)} %agg_ref.1, bf16[2,768,512]{2,1,0:T(8,128)(2,1)} %w_ref.1), custom_call_target="tpu_custom_call" | custom-call | tf_op jit(solution)/shard_map/pallas_call | solution.py:84
  64.5 138.2 %shard_map.111 = (f32[2,768,512]{2,1,0:T(8,128)}, f32[512,128]{1,0:T(8,128)}, f32[512,512]{1,0:T(8,128)}, f32[153,1024]{1,0:T(8,128)}, f32[8,128]{1,0:T(8,128)}) custom-call(bf16[16,192,512]{2,1,0:T(8,128)(2,1)} %get-tuple-element.12.hidden, bf16[160,8192]{1,0:T(8,128)(2,1)} %pad.4.w_class, bf16[512,768]{1,0:T(8,128)(2,1)} %pad_maximum_fusion.w_all, ...), custom_call_target="tpu_custom_call" | custom-call | tf_op jit(solution)/shard_map/pallas_call | solution.py:418
  202.7 1.2 slice.11
  204.5 0.0 copy-start.3
  204.6 0.0 copy-start.1
  204.6 4.0 %copy.18 = f32[2,768,512]{2,1,0:T(8,128)} copy(f32[2,768,512]{2,1,0:T(8,128)} %get-tuple-element.26) | data formatting | bytes 6291456
  208.5 0.0 copy-done.3
  208.5 0.0 copy-start.2
  208.5 0.7 copy.19
  209.2 0.0 copy-done.1
  209.2 1.0 copy.20
  210.2 0.0 copy-done.2
  210.2 0.8 copy.21
Async XLA Ops:
  0.6 4.5 %copy-start.5 = (s32[1536]{0:T(1024)S(1)}, s32[1536]{0:T(1024)}, u32[]{:S(2)}) copy-start(s32[1536]{0:T(1024)} %param.9) | copy-start | bytes 18436
  0.6 3.4 %copy-start.4 = (s32[1536]{0:T(1024)S(1)}, s32[1536]{0:T(1024)}, u32[]{:S(2)}) copy-start(s32[1536]{0:T(1024)} %param.8) | copy-start | bytes 18436
  1.7 4.6 %copy-start = (bf16[153,8192]{1,0:T(8,128)(2,1)S(1)}, bf16[153,8192]{1,0:T(8,128)(2,1)}, u32[]{:S(2)}) copy-start(bf16[153,8192]{1,0:T(8,128)(2,1)} %param.13) | copy-start | bytes 7520260
  204.5 4.0 %copy-start.3 = (f32[512,128]{1,0:T(8,128)S(1)}, f32[512,128]{1,0:T(8,128)}, u32[]{:S(2)}) copy-start(f32[512,128]{1,0:T(8,128)} %get-tuple-element.27) | copy-start | bytes 786436
  204.6 4.7 %copy-start.1 = (f32[512,512]{1,0:T(8,128)S(1)}, f32[512,512]{1,0:T(8,128)}, u32[]{:S(2)}) copy-start(f32[512,512]{1,0:T(8,128)} %get-tuple-element.28) | copy-start | bytes 3145732
  208.5 1.7 copy-start.2

commit v2 on v0

v2 whole, which is shorter than its diff:
```python
import functools

import jax
import jax.numpy as jnp
from jax import lax
from jax.experimental import pallas as pl
from jax.experimental.pallas import tpu as pltpu
from jax.sharding import PartitionSpec as P

MESH = pl.DeviceIdType.MESH
F32 = jnp.float32
BF16 = jnp.bfloat16
GROUPS = 8
CHIPS = 8
PAPERS = 192
HALF = 96
BLOCK = 16
METAS = 16
KEY = 64
CLASS_PAD = 160
TAIL = CLASS_PAD - 128


def dot(a, b):
    return jnp.dot(a, b, preferred_element_type=F32)


def dot_nt(a, b):
    return lax.dot_general(a, b, (((1,), (1,)), ((), ())), preferred_element_type=F32)


def dot_tn(a, b):
    return lax.dot_general(a, b, (((0,), (0,)), ((), ())), preferred_element_type=F32)


def iota(shape, axis):
    return lax.broadcasted_iota(jnp.int32, shape, axis)


def where_one(mask):
    return mask.astype(F32).astype(BF16)


def remote(src, dst, send_sem, recv_sem, where):
    return pltpu.make_async_remote_copy(
        src_ref=src, dst_ref=dst, send_sem=send_sem, recv_sem=recv_sem, device_id=where, device_id_type=MESH
    )


def step_kernel(
    seed, class_count,
    ids_ref, labels_ref, agg_hbm, w_proj, w_qk, w_value, w_class,
    gp_all, cls_all, qv_all, loss_node,
    agg, agg_sem, ids, labels, gathered, outbox, hidden, w_all, w_mix,
    joined, d_joined, values, attention, kq, dlogits, attended, mail, mail_in, d_qk, d_qk_in, spread_x,
    cls, cls_in, cls_chip, cls_g, cls_meta,
    qv_acc, qv, qv_in, qv_chip, qv_meta,
    gp, gp_in, gp_chip, loss_acc, loss_meta,
    out_sem, in_sem, mail_send, mail_recv, send_sem, recv_sem, sib_send, sib_recv,
):
    me = lax.axis_index("meta")
    node = lax.axis_index("node")
    chip, core = node // 2, lax.rem(node, 2)
    other = 1 - core
    sibling = {"node": 2 * chip + other}
    groups = [lax.rem(me + j, GROUPS) for j in range(1, GROUPS)]
    chips = [lax.rem(chip + j, CHIPS) for j in range(1, CHIPS)]
    width = w_value.shape[0]
    rows = agg.shape[1]
    feat = agg.shape[2]

    loads = [pltpu.make_async_copy(agg_hbm.at[m], agg.at[m], agg_sem.at[m]) for m in range(2)]
    for load in loads:
        load.start()

    barrier = pltpu.get_barrier_semaphore()
    for g in groups:
        pl.semaphore_signal(barrier, inc=1, device_id={"meta": g}, device_id_type=MESH)
    for k in chips:
        pl.semaphore_signal(barrier, inc=1, device_id={"node": 2 * k + core}, device_id_type=MESH)
    pl.semaphore_signal(barrier, inc=1, device_id=sibling, device_id_type=MESH)

    def to_group(phase, g, src, dst):
        return remote(src, dst, send_sem.at[phase, g], recv_sem.at[phase, me], {"meta": g})

    def from_group(phase, g, dst):
        return remote(dst, dst, send_sem.at[phase, g], recv_sem.at[phase, g], {"meta": g})

    def to_chip(phase, k, src, dst):
        return remote(src, dst, send_sem.at[phase, k], recv_sem.at[phase, chip], {"node": 2 * k + core})

    def from_chip(phase, k, dst):
        return remote(dst, dst, send_sem.at[phase, k], recv_sem.at[phase, k], {"node": 2 * k + core})

    def to_sibling(phase, src, dst):
        return remote(src, dst, sib_send.at[phase], sib_recv.at[phase], sibling)

    eye = iota((128, 128), 0) == iota((128, 128), 1)
    for t in range(ids_ref.shape[0]):
        for src, dst in ((ids_ref, ids), (labels_ref, labels)):
            row = jnp.broadcast_to(src[t : t + 1, :].astype(F32), (128, 128))
            dst[t * 128 : (t + 1) * 128, :] = jnp.sum(jnp.where(eye, row, 0.0), axis=1, keepdims=True).astype(jnp.int32)

    loads[0].wait()
    loads[1].wait()
    pl.semaphore_wait(barrier, GROUPS - 1 + CHIPS)

    def part(h):
        return pl.ds(pl.multiple_of(h * HALF, HALF), HALF)

    def out_copy(g, h, m):
        return remote(
            outbox.at[g, m, part(h), :],
            hidden.at[2 * me + m, part(h), :],
            out_sem.at[g, 2 * h + m],
            in_sem.at[me, 2 * h + m],
            {"meta": g},
        )

    def in_copy(g, h, m):
        here = hidden.at[2 * g + m, part(h), :]
        return remote(here, here, out_sem.at[g, 2 * h + m], in_sem.at[g, 2 * h + m], {"meta": g})

    def project_pair(p, h, with_own):
        first = lax.rem(me // 2 + p + 1, 4) * 2 + lax.rem(me + p, 2)
        second = lax.rem(me // 2 + 3 - p, 4) * 2 + lax.rem(me + p + 1, 2)
        if with_own:
            second = me
        spots = [pl.ds(pl.multiple_of(g * PAPERS + h * HALF, HALF), HALF) for g in (first, second)]
        column = jnp.concatenate([ids[spot, :] for spot in spots], axis=0)
        picks = where_one(column == iota((2 * HALF, rows), 1))
        for m in range(2):
            got = dot(picks, agg[m]).astype(BF16)
            row = dot(got, w_proj[m]).astype(BF16)
            for q, g in enumerate((first, second)):
                gathered[m, spots[q], :] = got[q * HALF : (q + 1) * HALF]
                mine = row[q * HALF : (q + 1) * HALF]
                outbox[g, m, part(h), :] = mine
                if with_own and q == 1:
                    hidden[2 * me + m, part(h), :] = mine
                else:
                    out_copy(g, h, m).start()

    def project_half(h, carry):
        def one(p, c):
            project_pair(p, h, False)
            return c

        lax.fori_loop(0, 3, one, 0)
        project_pair(3, h, True)
        return carry

    lax.fori_loop(0, 2, project_half, 0)

    swap = where_one(lax.rem(iota((2 * KEY, 2 * KEY), 0) + KEY, 2 * KEY) == iota((2 * KEY, 2 * KEY), 1))
    w_all[:, :width] = w_value[...]
    w_all[:, width : width + 2 * KEY] = w_qk[...]
    w_all[:, width + 2 * KEY :] = dot(w_qk[...], swap).astype(BF16)
    tail_at = 128 * METAS
    for m in range(METAS):
        lanes = slice(m * width, (m + 1) * width)
        w_mix[128 * m : 128 * (m + 1), :] = w_class[:128, lanes]
        last = w_class[128:class_count, lanes].astype(F32)
        zeros = jnp.zeros((CLASS_PAD - class_count, width), F32)
        w_mix[tail_at + TAIL * m : tail_at + TAIL * (m + 1), :] = jnp.concatenate([last, zeros], axis=0).astype(BF16)

    def class_rows(m):
        main = w_mix[pl.ds(pl.multiple_of(128 * m, 128), 128), :]
        tail = w_mix[pl.ds(pl.multiple_of(tail_at + TAIL * m, TAIL), TAIL), :]
        return jnp.concatenate([main, tail], axis=0)

    def class_rows_wide(m):
        return jnp.concatenate([class_rows(m), jnp.zeros((256 - CLASS_PAD, width), BF16)], axis=0)

    scale = KEY ** (-0.5)
    side = BLOCK * METAS
    same = lax.rem(iota((side, side), 0), BLOCK) == lax.rem(iota((side, side), 1), BLOCK)
    first = iota((side, 2 * KEY), 1) < KEY
    by_key = where_one(iota((side, side), 0) // BLOCK == iota((side, side), 1) // BLOCK)
    by_query = iota((side, side), 0) // BLOCK == lax.rem(iota((side, side), 1), METAS)

    def mail_to(g, h):
        return remote(
            mail.at[g, part(h), :], mail_in.at[me, part(h), :], mail_send.at[g, h], mail_recv.at[me, h], {"meta": g}
        )

    def mail_from(g, h):
        here = mail_in.at[g, part(h), :]
        return remote(here, here, mail_send.at[g, h], mail_recv.at[g, h], {"meta": g})

    def keys_to(g, h):
        return remote(
            d_qk.at[pl.ds(2 * g, 2), part(h), :],
            d_qk_in.at[me, :, part(h), :],
            mail_send.at[g, 2 + h],
            mail_recv.at[me, 2 + h],
            {"meta": g},
        )

    def keys_from(g, h):
        here = d_qk_in.at[g, :, part(h), :]
        return remote(here, here, mail_send.at[g, 2 + h], mail_recv.at[g, 2 + h], {"meta": g})

    def head(h, carry):
        for g in groups:
            for m in range(2):
                in_copy(g, h, m).wait_recv()

        def forward(t, c):
            b = h * (HALF // BLOCK) + t
            at = pl.ds(pl.multiple_of(b * BLOCK, BLOCK), BLOCK)
            here = hidden[:, at, :].reshape(side, width)
            mixed = dot(here, w_all[...]).astype(BF16)
            v = mixed[:, :width]
            swapped = mixed[:, width + 2 * KEY :]
            values[b] = v
            kq[b] = swapped
            q = jnp.where(first, mixed[:, width : width + 2 * KEY].astype(F32), 0.0).astype(BF16)
            scores = dot_nt(q, swapped) * scale
            weights = jnp.where(same, jnp.exp(scores), 0.0)
            att = weights / jnp.sum(weights, axis=1, keepdims=True)
            attention[b] = att
            att = att.astype(BF16)
            out = (dot(att, v) + here.astype(F32)).astype(BF16)
            joined[:, at, :] = out.reshape(METAS, BLOCK, width)
            wide = jnp.where(by_query, dot(att, by_key), 0.0)
            attended[at, :] = jnp.sum(wide.reshape(METAS, BLOCK, side), axis=0).astype(BF16)
            return c

        lax.fori_loop(0, HALF // BLOCK, forward, 0)

        logits = lax.fori_loop(
            0,
            METAS,
            lambda m, t: t + dot_nt(joined[m, part(h), :], class_rows_wide(m)),
            jnp.zeros((HALF, 256), F32),
        )
        class_at = iota((HALF, 256), 1)
        exps = jnp.where(class_at < class_count, jnp.exp(logits), 0.0)
        total = jnp.sum(exps, axis=1, keepdims=True)
        own = pl.ds(pl.multiple_of(me * PAPERS + h * HALF, HALF), HALF)
        onehot = (labels[own, :] == class_at).astype(F32)
        loss_rows = jnp.log(total) - jnp.sum(onehot * logits, axis=1, keepdims=True)
        loss_acc[h] = jnp.zeros((8, 128), F32) + jnp.sum(loss_rows)
        dl = (seed * (exps / total - onehot)).astype(BF16)
        dlogits[part(h), :] = dl

        lane = iota((side, 128), 1)
        for j in range(GROUPS):
            g = lax.rem(me + j, GROUPS)
            choose = where_one(jnp.logical_and(iota((side, 128), 0) == lane + 2 * METAS * g - TAIL, lane >= TAIL) & (lane < TAIL + 2 * METAS))
            second = (dl[:, 128:].astype(F32) + dot(attended[part(h), :], choose)).astype(BF16)
            box = mail_in if j == 0 else mail
            box[g, part(h), :128] = dl[:, :128]
            box[g, part(h), 128:] = second
            if j:
                mail_to(g, h).start()

        def spread(m, c):
            d_joined[m, part(h), :] = dot(dl[:, :CLASS_PAD], class_rows(m)).astype(BF16)
            return c

        lax.fori_loop(0, METAS, spread, 0)

        def backward(t, c):
            b = h * (HALF // BLOCK) + t
            at = pl.ds(pl.multiple_of(b * BLOCK, BLOCK), BLOCK)
            dj = d_joined[:, at, :].reshape(side, width)
            att = attention[b]
            d_att = dot_nt(dj, values[b])
            mean = jnp.sum(att * d_att, axis=1, keepdims=True)
            d_scores = (att * (d_att - mean) * scale).astype(BF16)
            swapped = kq[b]
            grad = jnp.where(first, dot(d_scores, swapped), dot_tn(d_scores, swapped))
            d_qk[:, at, :] = grad.astype(BF16).reshape(METAS, BLOCK, 2 * KEY)
            return c

        lax.fori_loop(0, HALF // BLOCK, backward, 0)
        for g in groups:
            keys_to(g, h).start()
        for m in range(2):
            d_qk_in[me, m, part(h), :] = d_qk[2 * me + m, part(h), :]
        return carry

    lax.fori_loop(0, 2, head, 0)

    def classes(g, carry):
        for m in range(2):
            grad = dot_tn(dlogits[:, :CLASS_PAD], joined[2 * g + m]).astype(BF16)
            for q in range(4):
                for p in range(2):
                    cls[p, 4 * m + q, g] = grad[p * (CLASS_PAD // 2) : (p + 1) * (CLASS_PAD // 2), q * 128 : (q + 1) * 128]
        return carry

    lax.fori_loop(0, GROUPS, classes, 0)
    c0 = to_sibling(0, cls.at[other], cls_in)
    c0.start()

    d_values = joined
    d_hidden = d_joined
    for g in groups:
        for h in range(2):
            mail_from(g, h).wait_recv()
    tail_lane = iota((128, TAIL * METAS), 1)
    tail_row = iota((128, TAIL * METAS), 0)
    repeat = where_one((tail_row < TAIL) & (lax.rem(tail_lane, TAIL) == tail_row))
    widen = [where_one(tail_row == TAIL + METAS * j + tail_lane // TAIL) for j in range(2)]

    def home_values(j, carry):
        s = lax.rem(me + j, GROUPS)
        main = mail_in[s, :, :128].astype(F32)
        second = mail_in[s, :, 128:]
        second_f = second.astype(F32)
        tails = dot(second, repeat)
        for q in range(2):
            at = slice(q * PAPERS, (q + 1) * PAPERS)
            spread_x[at, tail_at:] = (tails * dot(second, widen[q])).astype(BF16)
            for i in range(METAS):
                lane = TAIL + METAS * q + i
                spread_x[at, 128 * i : 128 * (i + 1)] = (second_f[:, lane : lane + 1] * main).astype(BF16)
        grads = dot(spread_x[...], w_mix[...]).astype(BF16)
        for q in range(2):
            d_values[2 * s + q] = grads[q * PAPERS : (q + 1) * PAPERS]
        return carry

    lax.fori_loop(0, 2, home_values, 0)

    c0.wait_recv()

    def pair_class(k, carry):
        cls_in[k] = (cls[core, k].astype(F32) + cls_in[k].astype(F32)).astype(BF16)
        return carry

    lax.fori_loop(0, CHIPS, pair_class, 0)
    for k in chips:
        to_chip(1, k, cls_in.at[k], cls_chip.at[chip]).start()
    cls_chip[chip] = cls_in[chip]

    lax.fori_loop(2, GROUPS, home_values, 0)

    for g in groups:
        for h in range(2):
            keys_from(g, h).wait_recv()
    qv_acc[...] = jnp.zeros_like(qv_acc)

    def home_hidden(s, carry):
        letters = mail_in[s, :, :CLASS_PAD]
        for m in range(2):
            dv = d_values[2 * s + m]
            dk = d_qk_in[s, m]
            dj = dot(letters, class_rows(2 * me + m)).astype(BF16).astype(F32)
            grad = dj + dot_nt(dv, w_value[...]) + dot_nt(dk, w_qk[...])
            d_hidden[GROUPS * m + s] = grad.astype(BF16)
            qv_acc[...] += dot_tn(outbox[s, m], jnp.concatenate([dv, dk], axis=1))
        return carry

    lax.fori_loop(0, GROUPS, home_hidden, 0)

    part_feat = gp.shape[2]

    def project(m):
        back = d_hidden[pl.ds(GROUPS * m, GROUPS)].reshape(GROUPS * PAPERS, width)
        grad = dot_tn(gathered[m], back)
        for k in range(CHIPS):
            gp[m, k] = grad[k * part_feat : (k + 1) * part_feat].astype(BF16)

    project(other)
    g0 = to_sibling(2, gp.at[other], gp_in)
    g0.start()

    part_rows = qv.shape[2]
    for p in range(2):
        for k in range(CHIPS):
            start = (p * CHIPS + k) * part_rows
            qv[p, k] = qv_acc[start : start + part_rows, :].astype(BF16)
    q0 = to_sibling(1, qv.at[other], qv_in)
    q0.start()
    project(core)

    g0.wait_recv()

    def pair_proj(k, carry):
        gp_in[k] = (gp[core, k].astype(F32) + gp_in[k].astype(F32)).astype(BF16)
        return carry

    lax.fori_loop(0, CHIPS, pair_proj, 0)
    for k in chips:
        to_chip(9, k, gp_in.at[k], gp_chip.at[chip]).start()
    gp_chip[chip] = gp_in[chip]

    q0.wait_recv()

    def pair_qv(k, carry):
        qv_in[k] = (qv[core, k].astype(F32) + qv_in[k].astype(F32)).astype(BF16)
        return carry

    lax.fori_loop(0, CHIPS, pair_qv, 0)
    for k in chips:
        to_chip(2, k, qv_in.at[k], qv_chip.at[chip]).start()
    qv_chip[chip] = qv_in[chip]

    for k in chips:
        from_chip(1, k, cls_chip.at[k]).wait_recv()

    def chip_sum(g, carry):
        cls_g[g] = jnp.sum(cls_chip[:, g].astype(F32), axis=0).astype(BF16)
        return carry

    lax.fori_loop(0, GROUPS, chip_sum, 0)
    cls_meta[me] = cls_g[me]
    loss_meta[me] = loss_acc[0] + loss_acc[1]
    for g in groups:
        to_group(3, g, cls_g.at[g], cls_meta.at[me]).start()
        to_group(5, g, loss_meta.at[me], loss_meta.at[me]).start()

    for k in chips:
        from_chip(2, k, qv_chip.at[k]).wait_recv()
    qv_meta[me] = jnp.sum(qv_chip[...].astype(F32), axis=0).astype(BF16)
    for g in groups:
        to_group(4, g, qv_meta.at[me], qv_meta.at[me]).start()

    for k in chips:
        from_chip(9, k, gp_chip.at[k]).wait_recv()
    gp_all[core, chip] = jnp.sum(gp_chip[...].astype(F32), axis=0).astype(BF16)
    for k in chips:
        to_chip(10, k, gp_all.at[core, chip], gp_all.at[core, chip]).start()

    def across(k):
        here = gp_all.at[core, k]
        return remote(here, here, send_sem.at[11, k], recv_sem.at[11, k], sibling)

    def across_in(k):
        here = gp_all.at[other, k]
        return remote(here, here, send_sem.at[11, k], recv_sem.at[11, k], sibling)

    across(chip).start()

    for g in groups:
        from_group(3, g, cls_meta.at[g]).wait_recv()
        from_group(4, g, qv_meta.at[g]).wait_recv()
        from_group(5, g, loss_meta.at[g]).wait_recv()
    cls_all[core, chip] = jnp.sum(cls_meta[...].astype(F32), axis=0).astype(BF16)
    qv_all[core, chip] = jnp.sum(qv_meta[...].astype(F32), axis=0).astype(BF16)
    loss_node[core, chip] = jnp.sum(loss_meta[...], axis=0)
    for k in chips:
        to_chip(6, k, cls_all.at[core, chip], cls_all.at[core, chip]).start()
        to_chip(7, k, qv_all.at[core, chip], qv_all.at[core, chip]).start()
        to_chip(8, k, loss_node.at[core, chip], loss_node.at[core, chip]).start()

    for k in chips:
        from_chip(10, k, gp_all.at[core, k]).wait_recv()
        across(k).start()

    for k in chips:
        from_chip(6, k, cls_all.at[core, k]).wait_recv()
        from_chip(7, k, qv_all.at[core, k]).wait_recv()
        from_chip(8, k, loss_node.at[core, k]).wait_recv()
    finals = [
        to_sibling(3, cls_all.at[core], cls_all.at[core]),
        to_sibling(4, qv_all.at[core], qv_all.at[core]),
        to_sibling(5, loss_node.at[core], loss_node.at[core]),
    ]
    for copy in finals:
        copy.start()

    for k in [chip] + chips:
        across_in(k).wait_recv()
    remote(cls_all.at[other], cls_all.at[other], sib_send.at[3], sib_recv.at[3], sibling).wait_recv()
    remote(qv_all.at[other], qv_all.at[other], sib_send.at[4], sib_recv.at[4], sibling).wait_recv()
    remote(loss_node.at[other], loss_node.at[other], sib_send.at[5], sib_recv.at[5], sibling).wait_recv()

    c0.wait_send()
    q0.wait_send()
    g0.wait_send()
    for copy in finals:
        copy.wait_send()
    for g in groups:
        for h in range(2):
            for m in range(2):
                out_copy(g, h, m).wait_send()
            mail_to(g, h).wait_send()
            keys_to(g, h).wait_send()
        to_group(3, g, cls_g.at[g], cls_meta.at[me]).wait_send()
        to_group(4, g, qv_meta.at[me], qv_meta.at[me]).wait_send()
        to_group(5, g, loss_meta.at[me], loss_meta.at[me]).wait_send()
    for k in chips:
        to_chip(1, k, cls_in.at[k], cls_chip.at[chip]).wait_send()
        to_chip(2, k, qv_in.at[k], qv_chip.at[chip]).wait_send()
        to_chip(6, k, cls_all.at[core, chip], cls_all.at[core, chip]).wait_send()
        to_chip(7, k, qv_all.at[core, chip], qv_all.at[core, chip]).wait_send()
        to_chip(8, k, loss_node.at[core, chip], loss_node.at[core, chip]).wait_send()
        to_chip(9, k, gp_in.at[k], gp_chip.at[chip]).wait_send()
        to_chip(10, k, gp_all.at[core, chip], gp_all.at[core, chip]).wait_send()
    for k in [chip] + chips:
        across(k).wait_send()


def finish_kernel(batch_total, class_count, gp, cls, qv, loss, proj_out, qk_out, value_out, class_out, loss_out):
    part_feat, width = gp.shape[2], gp.shape[3]
    part_rows = qv.shape[2]
    half_rows = cls.shape[2]
    for p in range(2):
        for k in range(CHIPS):
            proj_out[p, k * part_feat : (k + 1) * part_feat, :] = gp[p, k].astype(F32)
            start = (p * CHIPS + k) * part_rows
            block = qv[p, k].astype(F32)
            value_out[start : start + part_rows, :] = block[:, :width]
            qk_out[start : start + part_rows, :] = block[:, width:]
            lanes = slice(k * 128, (k + 1) * 128)
            if p == 0:
                class_out[:half_rows, lanes] = cls[0, k].astype(F32)
            else:
                class_out[half_rows:, lanes] = cls[1, k].astype(F32)[: class_count - half_rows]
    loss_out[0, 0] = jnp.sum(loss[...].reshape(2 * CHIPS, 8, 128), axis=0)[0, 0] / batch_total


def local(aggregates, batch_ids, labels, w_proj, w_qk, w_value, w_class):
    batch_total = labels.shape[0] * lax.axis_size("node")
    class_count = w_class.shape[0]
    count, rows, feat = aggregates.shape
    batch = batch_ids.shape[0]
    width = w_value.shape[0]
    side = BLOCK * METAS
    blocks = PAPERS // BLOCK
    mixed = width + 2 * KEY
    half = CLASS_PAD // 2
    part = feat // CHIPS
    part_rows = width // (2 * CHIPS)
    vmem = pl.BlockSpec(memory_space=pltpu.VMEM)
    sums = pl.pallas_call(
        functools.partial(step_kernel, 1.0 / batch_total**0.5, class_count),
        out_shape=(
            jax.ShapeDtypeStruct((2, CHIPS, part, width), BF16),
            jax.ShapeDtypeStruct((2, CHIPS, half, 128), BF16),
            jax.ShapeDtypeStruct((2, CHIPS, part_rows, mixed), BF16),
            jax.ShapeDtypeStruct((2, CHIPS, 8, 128), F32),
        ),
        in_specs=[vmem, vmem, pl.BlockSpec(memory_space=pl.ANY)] + [vmem] * 4,
        out_specs=(vmem,) * 4,
        scratch_shapes=[
            pltpu.VMEM((count, rows, feat), BF16),
            pltpu.SemaphoreType.DMA((2,)),
            pltpu.VMEM((batch, 1), jnp.int32),
            pltpu.VMEM((batch, 1), jnp.int32),
            pltpu.VMEM((count, batch, feat), BF16),
            pltpu.VMEM((GROUPS, count, PAPERS, width), BF16),
            pltpu.VMEM((METAS, PAPERS, width), BF16),
            pltpu.VMEM((width, width + 4 * KEY), BF16),
            pltpu.VMEM((METAS * CLASS_PAD, width), BF16),
            pltpu.VMEM((METAS, PAPERS, width), BF16),
            pltpu.VMEM((METAS, PAPERS, width), BF16),
            pltpu.VMEM((blocks, side, width), BF16),
            pltpu.VMEM((blocks, side, side), F32),
            pltpu.VMEM((blocks, side, 2 * KEY), BF16),
            pltpu.VMEM((PAPERS, 256), BF16),
            pltpu.VMEM((PAPERS, side), BF16),
            pltpu.VMEM((GROUPS, PAPERS, 256), BF16),
            pltpu.VMEM((GROUPS, PAPERS, 256), BF16),
            pltpu.VMEM((METAS, PAPERS, 2 * KEY), BF16),
            pltpu.VMEM((GROUPS, count, PAPERS, 2 * KEY), BF16),
            pltpu.VMEM((2 * PAPERS, METAS * CLASS_PAD), BF16),
            pltpu.VMEM((2, CHIPS, GROUPS, half, 128), BF16),
            pltpu.VMEM((CHIPS, GROUPS, half, 128), BF16),
            pltpu.VMEM((CHIPS, GROUPS, half, 128), BF16),
            pltpu.VMEM((GROUPS, half, 128), BF16),
            pltpu.VMEM((GROUPS, half, 128), BF16),
            pltpu.VMEM((width, mixed), F32),
            pltpu.VMEM((2, CHIPS, part_rows, mixed), BF16),
            pltpu.VMEM((CHIPS, part_rows, mixed), BF16),
            pltpu.VMEM((CHIPS, part_rows, mixed), BF16),
            pltpu.VMEM((GROUPS, part_rows, mixed), BF16),
            pltpu.VMEM((2, CHIPS, part, width), BF16),
            pltpu.VMEM((CHIPS, part, width), BF16),
            pltpu.VMEM((CHIPS, part, width), BF16),
            pltpu.VMEM((2, 8, 128), F32),
            pltpu.VMEM((GROUPS, 8, 128), F32),
            pltpu.SemaphoreType.DMA((GROUPS, 4)),
            pltpu.SemaphoreType.DMA((GROUPS, 4)),
            pltpu.SemaphoreType.DMA((GROUPS, 4)),
            pltpu.SemaphoreType.DMA((GROUPS, 4)),
            pltpu.SemaphoreType.DMA((12, 8)),
            pltpu.SemaphoreType.DMA((12, 8)),
            pltpu.SemaphoreType.DMA((6,)),
            pltpu.SemaphoreType.DMA((6,)),
        ],
        compiler_params=pltpu.CompilerParams(
            collective_id=1, has_side_effects=True, vmem_limit_bytes=62 * 1024 * 1024
        ),
    )(
        batch_ids.reshape(batch // 128, 128), labels.reshape(batch // 128, 128), aggregates, w_proj, w_qk, w_value, w_class
    )
    grad_proj, grad_qk, grad_value, grad_class, loss = pl.pallas_call(
        functools.partial(finish_kernel, batch_total, class_count),
        out_shape=(
            jax.ShapeDtypeStruct((count, feat, width), F32),
            jax.ShapeDtypeStruct((width, 2 * KEY), F32),
            jax.ShapeDtypeStruct((width, width), F32),
            jax.ShapeDtypeStruct((class_count, count * width), F32),
            jax.ShapeDtypeStruct((1, 1), F32),
        ),
        in_specs=[vmem] * 4,
        out_specs=(vmem,) * 4 + (pl.BlockSpec(memory_space=pltpu.SMEM),),
        compiler_params=pltpu.CompilerParams(vmem_limit_bytes=32 * 1024 * 1024),
    )(*sums)
    return (grad_proj, grad_qk, grad_value, grad_class, loss.reshape(()))


def solution(mesh):
    in_specs = (P("meta", "node", None), P("node"), P("node"), P("meta", None, None), P(), P(), P())
    out_specs = (P("meta", None, None), P(), P(), P(None, "meta"), P())
    return jax.shard_map(local, mesh=mesh, in_specs=in_specs, out_specs=out_specs, check_vma=False)
```

time: 490 us -> 150 us (0.31); the launches traced: 484 us -> 149 us
  waiting for transfers between devices: 257 us -> 0 us
  Pallas kernels: 0 us -> 144 us
  blocking collectives: 66 us -> 0 us
  matrix products: 59.4 us -> 0 us
  local copies, waits for them, and re-layouts: 61.5 us -> 4.3 us
  between operations: 16.3 us -> 0.65 us
  starting transfers between devices: 13.2 us -> 0 us
  other arithmetic: 10.1 us -> 0 us
    psum x2 -> x0, waiting for transfers between devices: 185 us -> none  [the longest x1 121 us: local(): lax.psum(proj_part.astype(jnp.bfloat16), 'node').astype(jnp.float32)]
    pallas_call x0 -> x2, Pallas kernels: none -> 144 us  [the longest x1 142 us: local(): pl.pallas_call(functools.partial(step_kernel, 1.0 / batch_total ** 0.5, c...]
    all_to_all x2 -> x0, waiting for transfers between devices: 71.9 us -> none  [the longest x1 39.5 us: local(): lax.all_to_all(projected, 'meta', split_axis=1, concat_axis=0, tiled=True)]
    psum x1 -> x0, blocking collectives: 66 us -> none  [local(): lax.psum((grad_qk, grad_value, grad_class, loss_part), ('meta', 'node'))]
    dot_general x16 -> x0, matrix products: 58.2 us -> none  [product(): jnp.einsum(pattern, first_op, second_op, preferred_element_type=jnp.float32)]
    gather x1 -> x0, local copies, waits for them, and re-layouts: 20.3 us -> none  [local(): gathered = jnp.take(aggregates, batch_ids, axis=1)]
    convert_element_type x1 -> x0, local copies, waits for them, and re-layouts: 14.5 us -> none  [local(): projected = product('pbf,pfd->pbd', gathered, w_proj).astype(jnp.bfloat16)]
    all_to_all x2 -> x0, starting transfers between devices: 12.8 us -> none  [the longest x1 8.31 us: local(): lax.all_to_all(projected, 'meta', split_axis=1, concat_axis=0, tiled=True)]
  transfers between devices with their start and end apart: 4 -> 0, of which waited for: 4 -> 0; matrix products, arithmetic and copies ran while one was open for 7% -> 0% of each run, Pallas kernels for 0% -> 0%
where the time goes in v2:
time: 150 us; the launch traced here: 149 us
  Pallas kernels  144 us (96%)
  local copies, waits for them, and re-layouts  4.3 us (3%)
    pallas_call x1, Pallas kernels, local(): pl.pallas_call(functools.partial(step_kernel, 1.0 / batch_total ** 0.5, c...  142 us
    unnamed x8, local copies, waits for them, and re-layouts  4.3 us

profile of v2, /device:TPU:1, one launch (start us, length us, event | category | flops | bytes accessed | tf_op | source)
XLA Modules:
  0.0 149.3 jit_solution(8287169619070745550)
XLA Ops:
  0.6 141.7 %shard_map.110 = (bf16[2,8,96,512]{3,2,1,0:T(8,128)(2,1)}, bf16[2,8,80,128]{3,2,1,0:T(8,128)(2,1)}, bf16[2,8,32,640]{3,2,1,0:T(8,128)(2,1)}, f32[2,8,8,128]{3,2,1,0:T(8,128)}) custom-call(s32[12,128]{1,0:T(8,128)} %bitcast.3, s32[12,128]{1,0:T(8,128)} %bitcast.4, bf16[2,2048,768]{2,1,0:T(8,128)(2,1)} %agg_hbm.1, bf16[2,768,512]{2,1,0:T(8,128)(2,1)} %w_proj.1, ...), custom_call_target="tpu_custom_call" | custom-call | tf_op jit(solution)/shard_map/pallas_call | solution.py:530
  142.4 0.0 copy-start
  142.4 1.4 copy-done
  143.8 0.0 copy-start.1
  143.8 1.1 copy-done.1
  144.9 0.0 copy-start.2
  144.9 1.0 copy-done.2
  145.8 0.0 copy-start.3
  145.8 0.8 copy-done.3
  146.7 2.7 %shard_map.111 = (f32[2,768,512]{2,1,0:T(8,128)}, f32[512,128]{1,0:T(8,128)}, f32[512,512]{1,0:T(8,128)}, f32[153,1024]{1,0:T(8,128)}, f32[1,1]{1,0:T(1,128)}) custom-call(bf16[2,8,96,512]{3,2,1,0:T(8,128)(2,1)S(1)} %copy-done, bf16[2,8,80,128]{3,2,1,0:T(8,128)(2,1)S(1)} %copy-done.2, bf16[2,8,32,640]{3,2,1,0:T(8,128)(2,1)S(1)} %copy-done.1, ...), custom_call_target="tpu_custom_call" | custom-call | tf_op jit(solution)/shard_map/pallas_call | solution.py:592
Async XLA Ops:
  142.4 1.4 copy-start
  143.8 1.1 copy-start.1
  144.9 1.0 copy-start.2
  145.8 0.8 copy-start.3

commit v3 on v2

v3 whole, which is shorter than its diff:
```python
import functools

import jax
import jax.numpy as jnp
from jax import lax
from jax.experimental import pallas as pl
from jax.experimental.pallas import tpu as pltpu
from jax.sharding import PartitionSpec as P

MESH = pl.DeviceIdType.MESH
F32 = jnp.float32
BF16 = jnp.bfloat16
GROUPS = 8
CHIPS = 8
PAPERS = 192
HALF = 96
BLOCK = 16
METAS = 16
KEY = 64
CLASS_PAD = 160
TAIL = CLASS_PAD - 128
UNROLL = 2


def dot(a, b):
    return jnp.dot(a, b, preferred_element_type=F32)


def dot_nt(a, b):
    return lax.dot_general(a, b, (((1,), (1,)), ((), ())), preferred_element_type=F32)


def dot_tn(a, b):
    return lax.dot_general(a, b, (((0,), (0,)), ((), ())), preferred_element_type=F32)


def iota(shape, axis):
    return lax.broadcasted_iota(jnp.int32, shape, axis)


def where_one(mask):
    return mask.astype(F32).astype(BF16)


def remote(src, dst, send_sem, recv_sem, where):
    return pltpu.make_async_remote_copy(
        src_ref=src, dst_ref=dst, send_sem=send_sem, recv_sem=recv_sem, device_id=where, device_id_type=MESH
    )


def step_kernel(
    seed, class_count,
    ids_ref, labels_ref, agg_hbm, w_proj_hbm, w_qk, w_value, w_class_hbm,
    gp_all, cls_all, qv_all, loss_node,
    load_sem, labels, gathered, outbox, hidden, w_all, w_back, w_mix,
    joined, d_joined, values, attention, kq, dlogits, attended, mail, mail_in, d_qk, d_vk,
    cls, cls_in, cls_meta, cls_k, cls_chip,
    qv, qv_in, qv_chip, qv_meta,
    gp, gp_in, gp_chip, loss_acc, loss_meta,
    out_sem, in_sem, mail_send, mail_recv, send_sem, recv_sem, sib_send, sib_recv,
):
    me = lax.axis_index("meta")
    node = lax.axis_index("node")
    chip, core = node // 2, lax.rem(node, 2)
    other = 1 - core
    sibling = {"node": 2 * chip + other}
    groups = [lax.rem(me + j, GROUPS) for j in range(1, GROUPS)]
    chips = [lax.rem(chip + j, CHIPS) for j in range(1, CHIPS)]
    width = w_value.shape[0]
    rows, feat = agg_hbm.shape[1:]
    tail_at = 128 * METAS

    barrier = pltpu.get_barrier_semaphore()
    for g in groups:
        pl.semaphore_signal(barrier, inc=1, device_id={"meta": g}, device_id_type=MESH)
    for k in chips:
        pl.semaphore_signal(barrier, inc=1, device_id={"node": 2 * k + core}, device_id_type=MESH)
    pl.semaphore_signal(barrier, inc=1, device_id=sibling, device_id_type=MESH)

    def to_group(phase, g, src, dst):
        return remote(src, dst, send_sem.at[phase, g], recv_sem.at[phase, me], {"meta": g})

    def from_group(phase, g, dst):
        return remote(dst, dst, send_sem.at[phase, g], recv_sem.at[phase, g], {"meta": g})

    def to_chip(phase, k, src, dst):
        return remote(src, dst, send_sem.at[phase, k], recv_sem.at[phase, chip], {"node": 2 * k + core})

    def from_chip(phase, k, dst):
        return remote(dst, dst, send_sem.at[phase, k], recv_sem.at[phase, k], {"node": 2 * k + core})

    def to_sibling(phase, src, dst):
        return remote(src, dst, sib_send.at[phase], sib_recv.at[phase], sibling)

    def to_column(src, dst):
        eye = iota((128, 128), 0) == iota((128, 128), 1)
        for t in range(src.shape[0]):
            row = jnp.broadcast_to(src[t : t + 1, :].astype(F32), (128, 128))
            dst[t * 128 : (t + 1) * 128, :] = jnp.sum(jnp.where(eye, row, 0.0), axis=1, keepdims=True).astype(jnp.int32)

    def part(h):
        return pl.ds(pl.multiple_of(h * HALF, HALF), HALF)

    def out_copy(g, h, m):
        return remote(
            outbox.at[m, g, part(h), :],
            hidden.at[2 * me + m, part(h), :],
            out_sem.at[g, 2 * h + m],
            in_sem.at[me, 2 * h + m],
            {"meta": g},
        )

    def in_copy(g, h, m):
        here = hidden.at[2 * g + m, part(h), :]
        return remote(here, here, out_sem.at[g, 2 * h + m], in_sem.at[g, 2 * h + m], {"meta": g})

    def front(agg, w_proj, w_class, ids):
        loads = []
        step = rows // 4
        for m in range(2):
            for q in range(4):
                at = pl.ds(q * step, step)
                loads.append(pltpu.make_async_copy(agg_hbm.at[m, at, :], agg.at[m, at, :], load_sem.at[4 * m + q]))
        loads.append(pltpu.make_async_copy(w_proj_hbm, w_proj, load_sem.at[8]))
        loads.append(pltpu.make_async_copy(w_class_hbm, w_class, load_sem.at[9]))
        for load in loads:
            load.start()
        to_column(ids_ref, ids)
        for load in loads[:9]:
            load.wait()
        pl.semaphore_wait(barrier, GROUPS - 1 + CHIPS)

        def project_pair(p, h, with_own):
            first = lax.rem(me // 2 + p + 1, 4) * 2 + lax.rem(me + p, 2)
            second = lax.rem(me // 2 + 3 - p, 4) * 2 + lax.rem(me + p + 1, 2)
            if with_own:
                second = me
            spots = [pl.ds(pl.multiple_of(g * PAPERS + h * HALF, HALF), HALF) for g in (first, second)]
            column = jnp.concatenate([ids[spot, :] for spot in spots], axis=0)
            picks = where_one(column == iota((2 * HALF, rows), 1))
            for m in range(2):
                got = dot(picks, agg[m]).astype(BF16)
                row = dot(got, w_proj[m]).astype(BF16)
                for q, g in enumerate((first, second)):
                    gathered[m, spots[q], :] = got[q * HALF : (q + 1) * HALF]
                    mine = row[q * HALF : (q + 1) * HALF]
                    outbox[m, g, part(h), :] = mine
                    if with_own and q == 1:
                        hidden[2 * me + m, part(h), :] = mine
                    else:
                        out_copy(g, h, m).start()

        def project_half(h, carry):
            def one(p, c):
                project_pair(p, h, False)
                return c

            lax.fori_loop(0, 3, one, 0)
            project_pair(3, h, True)
            return carry

        lax.fori_loop(0, 2, project_half, 0)

        swap = where_one(lax.rem(iota((2 * KEY, 2 * KEY), 0) + KEY, 2 * KEY) == iota((2 * KEY, 2 * KEY), 1))
        w_all[:, :width] = w_value[...]
        w_all[:, width : width + 2 * KEY] = w_qk[...]
        w_all[:, width + 2 * KEY :] = dot(w_qk[...], swap).astype(BF16)
        w_back[:width, :] = w_value[...].astype(F32).T.astype(BF16)
        w_back[width:, :] = w_qk[...].astype(F32).T.astype(BF16)
        loads[9].wait()
        for m in range(METAS):
            lanes = slice(m * width, (m + 1) * width)
            w_mix[128 * m : 128 * (m + 1), :] = w_class[:128, lanes]
            last = w_class[128:class_count, lanes].astype(F32)
            zeros = jnp.zeros((CLASS_PAD - class_count, width), F32)
            w_mix[tail_at + TAIL * m : tail_at + TAIL * (m + 1), :] = jnp.concatenate([last, zeros], axis=0).astype(BF16)

    pl.run_scoped(
        front,
        pltpu.VMEM(agg_hbm.shape, BF16),
        pltpu.VMEM(w_proj_hbm.shape, BF16),
        pltpu.VMEM(w_class_hbm.shape, BF16),
        pltpu.VMEM((GROUPS * PAPERS, 1), jnp.int32),
    )
    to_column(labels_ref, labels)

    def class_rows(m):
        main = w_mix[pl.ds(pl.multiple_of(128 * m, 128), 128), :]
        tail = w_mix[pl.ds(pl.multiple_of(tail_at + TAIL * m, TAIL), TAIL), :]
        return jnp.concatenate([main, tail], axis=0)

    def class_rows_wide(m):
        return jnp.concatenate([class_rows(m), jnp.zeros((256 - CLASS_PAD, width), BF16)], axis=0)

    scale = KEY ** (-0.5)
    side = BLOCK * METAS
    same = lax.rem(iota((side, side), 0), BLOCK) == lax.rem(iota((side, side), 1), BLOCK)
    first = iota((side, 2 * KEY), 1) < KEY
    by_key = where_one(iota((side, side), 0) // BLOCK == iota((side, side), 1) // BLOCK)
    by_query = iota((side, side), 0) // BLOCK == lax.rem(iota((side, side), 1), METAS)

    def mail_to(g, h):
        return remote(
            mail.at[g, part(h), :], mail_in.at[me, part(h), :], mail_send.at[g, h], mail_recv.at[me, h], {"meta": g}
        )

    def mail_from(g, h):
        here = mail_in.at[g, part(h), :]
        return remote(here, here, mail_send.at[g, h], mail_recv.at[g, h], {"meta": g})

    def key_rows(g, h):
        return pl.ds(pl.multiple_of(g * PAPERS + h * HALF, HALF), HALF)

    def keys_to(g, h):
        return remote(
            d_qk.at[pl.ds(2 * g, 2), part(h), :],
            d_vk.at[:, key_rows(me, h), pl.ds(width, 2 * KEY)],
            mail_send.at[g, 2 + h],
            mail_recv.at[me, 2 + h],
            {"meta": g},
        )

    def keys_from(g, h):
        here = d_vk.at[:, key_rows(g, h), pl.ds(width, 2 * KEY)]
        return remote(here, here, mail_send.at[g, 2 + h], mail_recv.at[g, 2 + h], {"meta": g})

    def head(h, carry):
        for g in groups:
            for m in range(2):
                in_copy(g, h, m).wait_recv()

        def forward(t, c):
            b = h * (HALF // BLOCK) + t
            at = pl.ds(pl.multiple_of(b * BLOCK, BLOCK), BLOCK)
            here = hidden[:, at, :].reshape(side, width)
            mixed = dot(here, w_all[...]).astype(BF16)
            v = mixed[:, :width]
            swapped = mixed[:, width + 2 * KEY :]
            values[b] = v
            kq[b] = swapped
            q = jnp.where(first, mixed[:, width : width + 2 * KEY].astype(F32), 0.0).astype(BF16)
            scores = dot_nt(q, swapped) * scale
            weights = jnp.where(same, jnp.exp(scores), 0.0)
            att = weights * (1.0 / jnp.sum(weights, axis=1, keepdims=True))
            attention[b] = att
            att = att.astype(BF16)
            out = (dot(att, v) + here.astype(F32)).astype(BF16)
            joined[:, at, :] = out.reshape(METAS, BLOCK, width)
            wide = jnp.where(by_query, dot(att, by_key), 0.0)
            attended[at, :] = jnp.sum(wide.reshape(METAS, BLOCK, side), axis=0).astype(BF16)
            return c

        lax.fori_loop(0, HALF // BLOCK, forward, 0, unroll=UNROLL)

        logits = lax.fori_loop(
            0,
            METAS,
            lambda m, t: t + dot_nt(joined[m, part(h), :], class_rows_wide(m)),
            jnp.zeros((HALF, 256), F32),
        )
        class_at = iota((HALF, 256), 1)
        exps = jnp.where(class_at < class_count, jnp.exp(logits), 0.0)
        total = jnp.sum(exps, axis=1, keepdims=True)
        own = pl.ds(pl.multiple_of(me * PAPERS + h * HALF, HALF), HALF)
        onehot = (labels[own, :] == class_at).astype(F32)
        loss_rows = jnp.log(total) - jnp.sum(onehot * logits, axis=1, keepdims=True)
        loss_acc[h] = jnp.zeros((8, 128), F32) + jnp.sum(loss_rows)
        dl = (seed * (exps / total - onehot)).astype(BF16)
        dlogits[part(h), :] = dl

        lane = iota((side, 128), 1)
        for j in range(GROUPS):
            g = lax.rem(me + j, GROUPS)
            choose = where_one(jnp.logical_and(iota((side, 128), 0) == lane + 2 * METAS * g - TAIL, lane >= TAIL) & (lane < TAIL + 2 * METAS))
            second = (dl[:, 128:].astype(F32) + dot(attended[part(h), :], choose)).astype(BF16)
            box = mail_in if j == 0 else mail
            box[g, part(h), :128] = dl[:, :128]
            box[g, part(h), 128:] = second
            if j:
                mail_to(g, h).start()

        def spread(m, c):
            d_joined[m, part(h), :] = dot(dl[:, :CLASS_PAD], class_rows(m)).astype(BF16)
            return c

        lax.fori_loop(0, METAS, spread, 0)

        def backward(t, c):
            b = h * (HALF // BLOCK) + t
            at = pl.ds(pl.multiple_of(b * BLOCK, BLOCK), BLOCK)
            dj = d_joined[:, at, :].reshape(side, width)
            att = attention[b]
            d_att = dot_nt(dj, values[b])
            mean = jnp.sum(att * d_att, axis=1, keepdims=True)
            d_scores = (att * (d_att - mean) * scale).astype(BF16)
            swapped = kq[b]
            grad = jnp.where(first, dot(d_scores, swapped), dot_tn(d_scores, swapped))
            d_qk[:, at, :] = grad.astype(BF16).reshape(METAS, BLOCK, 2 * KEY)
            return c

        lax.fori_loop(0, HALF // BLOCK, backward, 0, unroll=UNROLL)
        for g in groups:
            keys_to(g, h).start()
        for m in range(2):
            d_vk[m, key_rows(me, h), width:] = d_qk[2 * me + m, part(h), :]
        return carry

    lax.fori_loop(0, 2, head, 0)

    def classes(g, carry):
        for m in range(2):
            grad = dot_tn(dlogits[:, :CLASS_PAD], joined[2 * g + m]).astype(BF16)
            for q in range(4):
                for p in range(2):
                    cls[p, g, 4 * m + q] = grad[p * (CLASS_PAD // 2) : (p + 1) * (CLASS_PAD // 2), q * 128 : (q + 1) * 128]
        return carry

    lax.fori_loop(0, GROUPS, classes, 0)
    c0 = to_sibling(0, cls.at[other], cls_in)
    c0.start()

    for g in groups:
        for h in range(2):
            mail_from(g, h).wait_recv()
    c0.wait_recv()

    def pair_class(g, carry):
        cls_in[g] = (cls[core, g].astype(F32) + cls_in[g].astype(F32)).astype(BF16)
        return carry

    lax.fori_loop(0, GROUPS, pair_class, 0)
    for g in groups:
        to_group(1, g, cls_in.at[g], cls_meta.at[me]).start()
    cls_meta[me] = cls_in[me]

    tail_lane = iota((128, TAIL * METAS), 1)
    tail_row = iota((128, TAIL * METAS), 0)
    repeat = where_one((tail_row < TAIL) & (lax.rem(tail_lane, TAIL) == tail_row))
    widen = [where_one(tail_row == TAIL + METAS * j + tail_lane // TAIL) for j in range(2)]

    def home_values(x_even, x_odd):
        def build(j, x):
            s = lax.rem(me + j, GROUPS)
            main = mail_in[s, :, :128].astype(F32)
            second = mail_in[s, :, 128:]
            second_f = second.astype(F32)
            tails = dot(second, repeat)
            for q in range(2):
                at = slice(q * PAPERS, (q + 1) * PAPERS)
                x[at, tail_at:] = (tails * dot(second, widen[q])).astype(BF16)
                for i in range(METAS):
                    lane = TAIL + METAS * q + i
                    x[at, 128 * i : 128 * (i + 1)] = (second_f[:, lane : lane + 1] * main).astype(BF16)

        def multiply(j, x):
            s = lax.rem(me + j, GROUPS)
            grads = dot(x[...], w_mix[...]).astype(BF16)
            for q in range(2):
                at = pl.ds(pl.multiple_of(s * PAPERS, PAPERS), PAPERS)
                d_vk[q, at, :width] = grads[q * PAPERS : (q + 1) * PAPERS]

        build(0, x_even)

        def two(t, carry):
            build(2 * t + 1, x_odd)
            multiply(2 * t, x_even)
            build(2 * t + 2, x_even)
            multiply(2 * t + 1, x_odd)
            return carry

        lax.fori_loop(0, GROUPS // 2, two, 0)

    spread_shape = pltpu.VMEM((2 * PAPERS, METAS * CLASS_PAD), BF16)
    pl.run_scoped(home_values, spread_shape, spread_shape)

    for g in groups:
        for h in range(2):
            keys_from(g, h).wait_recv()

    batch = GROUPS * PAPERS
    part_rows = qv.shape[2]
    for c in range(4):
        cols = slice(c * 128, (c + 1) * 128)
        grad = sum(dot_tn(outbox[m].reshape(batch, width)[:, cols], d_vk[m]) for m in range(2)).astype(BF16)
        for r in range(128 // part_rows):
            piece = c * (128 // part_rows) + r
            qv[piece // CHIPS, piece % CHIPS] = grad[r * part_rows : (r + 1) * part_rows]
    q0 = to_sibling(1, qv.at[other], qv_in)
    q0.start()

    d_hidden = d_joined

    def home_hidden(m):
        def some(r, carry):
            at = pl.ds(pl.multiple_of(r * 2 * PAPERS, 2 * PAPERS), 2 * PAPERS)
            letters = mail_in[pl.ds(2 * r, 2)].reshape(2 * PAPERS, 256)[:, :CLASS_PAD]
            grad = dot(letters, class_rows(2 * me + m)) + dot(d_vk[m, at, :], w_back[...])
            d_hidden[pl.ds(GROUPS * m + 2 * r, 2)] = grad.astype(BF16).reshape(2, PAPERS, width)
            return carry

        lax.fori_loop(0, GROUPS // 2, some, 0)

    part_feat = gp.shape[3]

    def project(m):
        back = d_hidden[GROUPS * m : GROUPS * (m + 1)].reshape(batch, width)
        grad = dot_tn(gathered[m], back)
        for p in range(2):
            for k in range(CHIPS):
                start = (p * CHIPS + k) * part_feat
                gp[m, p, k] = grad[start : start + part_feat].astype(BF16)

    def pair_proj(m):
        def one(k, carry):
            gp_in[m, k] = (gp[m, core, k].astype(F32) + gp_in[m, k].astype(F32)).astype(BF16)
            return carry

        lax.fori_loop(0, CHIPS, one, 0)
        for k in chips:
            to_chip(9 + m, k, gp_in.at[m, k], gp_chip.at[m, chip]).start()
        gp_chip[m, chip] = gp_in[m, chip]

    def across(m, k):
        here = gp_all.at[m, core, k]
        return remote(here, here, send_sem.at[13 + m, k], recv_sem.at[13 + m, k], sibling)

    def across_in(m, k):
        here = gp_all.at[m, other, k]
        return remote(here, here, send_sem.at[13 + m, k], recv_sem.at[13 + m, k], sibling)

    def chip_proj(m):
        for k in chips:
            from_chip(9 + m, k, gp_chip.at[m, k]).wait_recv()
        gp_all[m, core, chip] = jnp.sum(gp_chip[m].astype(F32), axis=0).astype(BF16)
        for k in chips:
            to_chip(11 + m, k, gp_all.at[m, core, chip], gp_all.at[m, core, chip]).start()
        across(m, chip).start()

    def pass_on(m):
        for k in chips:
            from_chip(11 + m, k, gp_all.at[m, core, k]).wait_recv()
            across(m, k).start()

    home_hidden(0)

    q0.wait_recv()

    def pair_qv(k, carry):
        qv_in[k] = (qv[core, k].astype(F32) + qv_in[k].astype(F32)).astype(BF16)
        return carry

    lax.fori_loop(0, CHIPS, pair_qv, 0)
    for k in chips:
        to_chip(2, k, qv_in.at[k], qv_chip.at[chip]).start()
    qv_chip[chip] = qv_in[chip]

    project(0)
    g0 = [to_sibling(2 + 4 * m, gp.at[m, other], gp_in.at[m]) for m in range(2)]
    g0[0].start()
    home_hidden(1)
    g0[0].wait_recv()
    pair_proj(0)
    project(1)
    g0[1].start()

    for k in chips:
        from_chip(2, k, qv_chip.at[k]).wait_recv()
    qv_meta[me] = jnp.sum(qv_chip[...].astype(F32), axis=0).astype(BF16)
    loss_meta[me] = loss_acc[0] + loss_acc[1]
    for g in groups:
        to_group(4, g, qv_meta.at[me], qv_meta.at[me]).start()
        to_group(5, g, loss_meta.at[me], loss_meta.at[me]).start()

    g0[1].wait_recv()
    pair_proj(1)

    for g in groups:
        from_group(1, g, cls_meta.at[g]).wait_recv()

    def meta_sum(k, carry):
        cls_k[k] = jnp.sum(cls_meta[:, k].astype(F32), axis=0).astype(BF16)
        return carry

    lax.fori_loop(0, CHIPS, meta_sum, 0)
    for k in chips:
        to_chip(3, k, cls_k.at[k], cls_chip.at[chip]).start()
    cls_chip[chip] = cls_k[chip]

    chip_proj(0)

    for g in groups:
        from_group(4, g, qv_meta.at[g]).wait_recv()
        from_group(5, g, loss_meta.at[g]).wait_recv()
    qv_all[core, chip] = jnp.sum(qv_meta[...].astype(F32), axis=0).astype(BF16)
    loss_node[core, chip] = jnp.sum(loss_meta[...], axis=0)
    for k in chips:
        to_chip(7, k, qv_all.at[core, chip], qv_all.at[core, chip]).start()
        to_chip(8, k, loss_node.at[core, chip], loss_node.at[core, chip]).start()

    chip_proj(1)

    for k in chips:
        from_chip(3, k, cls_chip.at[k]).wait_recv()
    cls_all[core, chip] = jnp.sum(cls_chip[...].astype(F32), axis=0).astype(BF16)
    for k in chips:
        to_chip(6, k, cls_all.at[core, chip], cls_all.at[core, chip]).start()

    pass_on(0)

    for k in chips:
        from_chip(6, k, cls_all.at[core, k]).wait_recv()
        from_chip(7, k, qv_all.at[core, k]).wait_recv()
        from_chip(8, k, loss_node.at[core, k]).wait_recv()
    finals = [
        to_sibling(3, cls_all.at[core], cls_all.at[core]),
        to_sibling(4, qv_all.at[core], qv_all.at[core]),
        to_sibling(5, loss_node.at[core], loss_node.at[core]),
    ]
    for copy in finals:
        copy.start()

    pass_on(1)

    for m in range(2):
        for k in [chip] + chips:
            across_in(m, k).wait_recv()
    remote(cls_all.at[other], cls_all.at[other], sib_send.at[3], sib_recv.at[3], sibling).wait_recv()
    remote(qv_all.at[other], qv_all.at[other], sib_send.at[4], sib_recv.at[4], sibling).wait_recv()
    remote(loss_node.at[other], loss_node.at[other], sib_send.at[5], sib_recv.at[5], sibling).wait_recv()

    c0.wait_send()
    q0.wait_send()
    for copy in g0 + finals:
        copy.wait_send()
    for g in groups:
        for h in range(2):
            for m in range(2):
                out_copy(g, h, m).wait_send()
            mail_to(g, h).wait_send()
            keys_to(g, h).wait_send()
        to_group(1, g, cls_in.at[g], cls_meta.at[me]).wait_send()
        to_group(4, g, qv_meta.at[me], qv_meta.at[me]).wait_send()
        to_group(5, g, loss_meta.at[me], loss_meta.at[me]).wait_send()
    for k in chips:
        to_chip(2, k, qv_in.at[k], qv_chip.at[chip]).wait_send()
        to_chip(3, k, cls_k.at[k], cls_chip.at[chip]).wait_send()
        to_chip(6, k, cls_all.at[core, chip], cls_all.at[core, chip]).wait_send()
        to_chip(7, k, qv_all.at[core, chip], qv_all.at[core, chip]).wait_send()
        to_chip(8, k, loss_node.at[core, chip], loss_node.at[core, chip]).wait_send()
    for m in range(2):
        for k in chips:
            to_chip(9 + m, k, gp_in.at[m, k], gp_chip.at[m, chip]).wait_send()
            to_chip(11 + m, k, gp_all.at[m, core, chip], gp_all.at[m, core, chip]).wait_send()
        for k in [chip] + chips:
            across(m, k).wait_send()


def finish_kernel(
    batch_total, class_count,
    gp_hbm, cls_hbm, qv_hbm, loss_hbm, proj_hbm, qk_out, value_out, class_out, loss_out,
    gp, cls, qv, loss, proj, in_sem, out_sem,
):
    part_feat, width = gp.shape[3:]
    part_rows = qv.shape[2]
    half_rows = cls.shape[2]
    loads = [pltpu.make_async_copy(gp_hbm.at[m], gp.at[m], in_sem.at[m]) for m in range(2)]
    for q, (src, dst) in enumerate(((cls_hbm, cls), (qv_hbm, qv), (loss_hbm, loss))):
        loads.append(pltpu.make_async_copy(src, dst, in_sem.at[2 + q]))
    for load in loads:
        load.start()
    stores = []
    for m in range(2):
        loads[m].wait()
        for p in range(2):
            for k in range(CHIPS):
                start = (p * CHIPS + k) * part_feat
                proj[m, start : start + part_feat, :] = gp[m, p, k].astype(F32)
        stores.append(pltpu.make_async_copy(proj.at[m], proj_hbm.at[m], out_sem.at[m]))
        stores[m].start()
    for load in loads[2:]:
        load.wait()
    for p in range(2):
        for k in range(CHIPS):
            start = (p * CHIPS + k) * part_rows
            block = qv[p, k].astype(F32)
            value_out[start : start + part_rows, :] = block[:, :width]
            qk_out[start : start + part_rows, :] = block[:, width:]
            lanes = slice(k * 128, (k + 1) * 128)
            if p == 0:
                class_out[:half_rows, lanes] = cls[0, k].astype(F32)
            else:
                class_out[half_rows:, lanes] = cls[1, k].astype(F32)[: class_count - half_rows]
    loss_out[0, 0] = jnp.sum(loss[...].reshape(2 * CHIPS, 8, 128), axis=0)[0, 0] / batch_total
    for store in stores:
        store.wait()


def local(aggregates, batch_ids, labels, w_proj, w_qk, w_value, w_class):
    batch_total = labels.shape[0] * lax.axis_size("node")
    class_count = w_class.shape[0]
    count, rows, feat = aggregates.shape
    batch = batch_ids.shape[0]
    width = w_value.shape[0]
    side = BLOCK * METAS
    blocks = PAPERS // BLOCK
    mixed = width + 2 * KEY
    half = CLASS_PAD // 2
    part = feat // (2 * CHIPS)
    part_rows = width // (2 * CHIPS)
    vmem = pl.BlockSpec(memory_space=pltpu.VMEM)
    anywhere = pl.BlockSpec(memory_space=pl.ANY)
    sums = pl.pallas_call(
        functools.partial(step_kernel, 1.0 / batch_total**0.5, class_count),
        out_shape=(
            jax.ShapeDtypeStruct((count, 2, CHIPS, part, width), BF16),
            jax.ShapeDtypeStruct((2, CHIPS, half, 128), BF16),
            jax.ShapeDtypeStruct((2, CHIPS, part_rows, mixed), BF16),
            jax.ShapeDtypeStruct((2, CHIPS, 8, 128), F32),
        ),
        in_specs=[vmem, vmem, anywhere, anywhere, vmem, vmem, anywhere],
        out_specs=(vmem,) * 4,
        scratch_shapes=[
            pltpu.SemaphoreType.DMA((10,)),
            pltpu.VMEM((batch, 1), jnp.int32),
            pltpu.VMEM((count, batch, feat), BF16),
            pltpu.VMEM((count, GROUPS, PAPERS, width), BF16),
            pltpu.VMEM((METAS, PAPERS, width), BF16),
            pltpu.VMEM((width, width + 4 * KEY), BF16),
            pltpu.VMEM((mixed, width), BF16),
            pltpu.VMEM((METAS * CLASS_PAD, width), BF16),
            pltpu.VMEM((METAS, PAPERS, width), BF16),
            pltpu.VMEM((METAS, PAPERS, width), BF16),
            pltpu.VMEM((blocks, side, width), BF16),
            pltpu.VMEM((blocks, side, side), F32),
            pltpu.VMEM((blocks, side, 2 * KEY), BF16),
            pltpu.VMEM((PAPERS, 256), BF16),
            pltpu.VMEM((PAPERS, side), BF16),
            pltpu.VMEM((GROUPS, PAPERS, 256), BF16),
            pltpu.VMEM((GROUPS, PAPERS, 256), BF16),
            pltpu.VMEM((METAS, PAPERS, 2 * KEY), BF16),
            pltpu.VMEM((count, batch, mixed), BF16),
            pltpu.VMEM((2, GROUPS, CHIPS, half, 128), BF16),
            pltpu.VMEM((GROUPS, CHIPS, half, 128), BF16),
            pltpu.VMEM((GROUPS, CHIPS, half, 128), BF16),
            pltpu.VMEM((CHIPS, half, 128), BF16),
            pltpu.VMEM((CHIPS, half, 128), BF16),
            pltpu.VMEM((2, CHIPS, part_rows, mixed), BF16),
            pltpu.VMEM((CHIPS, part_rows, mixed), BF16),
            pltpu.VMEM((CHIPS, part_rows, mixed), BF16),
            pltpu.VMEM((GROUPS, part_rows, mixed), BF16),
            pltpu.VMEM((count, 2, CHIPS, part, width), BF16),
            pltpu.VMEM((count, CHIPS, part, width), BF16),
            pltpu.VMEM((count, CHIPS, part, width), BF16),
            pltpu.VMEM((2, 8, 128), F32),
            pltpu.VMEM((GROUPS, 8, 128), F32),
            pltpu.SemaphoreType.DMA((GROUPS, 4)),
            pltpu.SemaphoreType.DMA((GROUPS, 4)),
            pltpu.SemaphoreType.DMA((GROUPS, 4)),
            pltpu.SemaphoreType.DMA((GROUPS, 4)),
            pltpu.SemaphoreType.DMA((15, 8)),
            pltpu.SemaphoreType.DMA((15, 8)),
            pltpu.SemaphoreType.DMA((7,)),
            pltpu.SemaphoreType.DMA((7,)),
        ],
        compiler_params=pltpu.CompilerParams(
            collective_id=1, has_side_effects=True, vmem_limit_bytes=62 * 1024 * 1024
        ),
    )(
        batch_ids.reshape(batch // 128, 128), labels.reshape(batch // 128, 128), aggregates, w_proj, w_qk, w_value, w_class
    )
    grad_proj, grad_qk, grad_value, grad_class, loss = pl.pallas_call(
        functools.partial(finish_kernel, batch_total, class_count),
        out_shape=(
            jax.ShapeDtypeStruct((count, feat, width), F32),
            jax.ShapeDtypeStruct((width, 2 * KEY), F32),
            jax.ShapeDtypeStruct((width, width), F32),
            jax.ShapeDtypeStruct((class_count, count * width), F32),
            jax.ShapeDtypeStruct((1, 1), F32),
        ),
        in_specs=[anywhere] * 4,
        out_specs=(anywhere,) + (vmem,) * 3 + (pl.BlockSpec(memory_space=pltpu.SMEM),),
        scratch_shapes=[
            pltpu.VMEM((count, 2, CHIPS, part, width), BF16),
            pltpu.VMEM((2, CHIPS, half, 128), BF16),
            pltpu.VMEM((2, CHIPS, part_rows, mixed), BF16),
            pltpu.VMEM((2, CHIPS, 8, 128), F32),
            pltpu.VMEM((count, feat, width), F32),
            pltpu.SemaphoreType.DMA((5,)),
            pltpu.SemaphoreType.DMA((2,)),
        ],
        compiler_params=pltpu.CompilerParams(vmem_limit_bytes=32 * 1024 * 1024),
    )(*sums)
    return (grad_proj, grad_qk, grad_value, grad_class, loss.reshape(()))


def solution(mesh):
    in_specs = (P("meta", "node", None), P("node"), P("node"), P("meta", None, None), P(), P(), P())
    out_specs = (P("meta", None, None), P(), P(), P(None, "meta"), P())
    return jax.shard_map(local, mesh=mesh, in_specs=in_specs, out_specs=out_specs, check_vma=False)
```

time: 150 us -> 145 us (0.967)
  Pallas kernels: 144 us -> 139 us
    pallas_call x1, Pallas kernels: 142 us -> 135 us  [local(): pl.pallas_call(functools.partial(step_kernel, 1.0 / batch_total ** 0.5, c...]
where the time goes in v3:
time: 145 us; the launch traced here: 144 us
  Pallas kernels  139 us (96%)
  local copies, waits for them, and re-layouts  4.3 us (3%)
    pallas_call x1, Pallas kernels, local(): pl.pallas_call(functools.partial(step_kernel, 1.0 / batch_total ** 0.5, c...  135 us
    unnamed x8, local copies, waits for them, and re-layouts  4.3 us
    pallas_call x1, Pallas kernels, local(): pl.pallas_call(functools.partial(finish_kernel, batch_total, class_count)...  3.59 us

profile of v3, /device:TPU:1, one launch (start us, length us, event | category | flops | bytes accessed | tf_op | source)
XLA Modules:
  0.0 143.9 jit_solution(2752120786929185730)
XLA Ops:
  0.6 135.2 %shard_map.110 = (bf16[2,2,8,48,512]{4,3,2,1,0:T(8,128)(2,1)}, bf16[2,8,80,128]{3,2,1,0:T(8,128)(2,1)}, bf16[2,8,32,640]{3,2,1,0:T(8,128)(2,1)}, f32[2,8,8,128]{3,2,1,0:T(8,128)}) custom-call(s32[12,128]{1,0:T(8,128)} %bitcast.3, s32[12,128]{1,0:T(8,128)} %bitcast.4, bf16[2,2048,768]{2,1,0:T(8,128)(2,1)} %agg_hbm.1, bf16[2,768,512]{2,1,0:T(8,128)(2,1)} %w_proj_hbm.1, ...), custom_call_target="tpu_custom_call" | custom-call | tf_op jit(solution)/shard_map/pallas_call | solution.py:612
  135.9 0.0 copy-start
  135.9 1.4 copy-done
  137.3 0.0 copy-start.1
  137.3 1.1 copy-done.1
  138.4 0.0 copy-start.2
  138.4 1.0 copy-done.2
  139.3 0.0 copy-start.3
  139.3 0.8 copy-done.3
  140.2 3.6 %shard_map.111 = (f32[2,768,512]{2,1,0:T(8,128)}, f32[512,128]{1,0:T(8,128)}, f32[512,512]{1,0:T(8,128)}, f32[153,1024]{1,0:T(8,128)}, f32[1,1]{1,0:T(1,128)}) custom-call(bf16[2,2,8,48,512]{4,3,2,1,0:T(8,128)(2,1)S(1)} %copy-done, bf16[2,8,80,128]{3,2,1,0:T(8,128)(2,1)S(1)} %copy-done.2, bf16[2,8,32,640]{3,2,1,0:T(8,128)(2,1)S(1)} %copy-done.1, ...), custom_call_target="tpu_custom_call" | custom-call | tf_op jit(solution)/shard_map/pallas_call | solution.py:671
Async XLA Ops:
  135.9 1.4 copy-start
  137.3 1.1 copy-start.1
  138.4 1.0 copy-start.2
  139.3 0.8 copy-start.3

commit v4 on v3

--- a/solution.py
+++ b/solution.py
@@ -19,7 +19,8 @@
 KEY = 64
 CLASS_PAD = 160
 TAIL = CLASS_PAD - 128
-UNROLL = 2
+META_ROWS = 48
+UNROLL = 6
 
 
 def dot(a, b):
@@ -53,8 +54,8 @@
     ids_ref, labels_ref, agg_hbm, w_proj_hbm, w_qk, w_value, w_class_hbm,
     gp_all, cls_all, qv_all, loss_node,
     load_sem, labels, gathered, outbox, hidden, w_all, w_back, w_mix,
-    joined, d_joined, values, attention, kq, dlogits, attended, mail, mail_in, d_qk, d_vk,
-    cls, cls_in, cls_meta, cls_k, cls_chip,
+    joined, d_joined, dlogits, attended, mail, mail_in, d_vq, d_vk,
+    cx, cx_in, cx_meta, cx_sum, cx_chip, cy, cy_in, cy_chip, cy_sum, cy_meta,
     qv, qv_in, qv_chip, qv_meta,
     gp, gp_in, gp_chip, loss_acc, loss_meta,
     out_sem, in_sem, mail_send, mail_recv, send_sem, recv_sem, sib_send, sib_recv,
@@ -161,6 +162,9 @@
 
         lax.fori_loop(0, 2, project_half, 0)
 
+        to_column(labels_ref, ids)
+        labels[...] = ids[pl.ds(pl.multiple_of(me * PAPERS, PAPERS), PAPERS), :]
+
         swap = where_one(lax.rem(iota((2 * KEY, 2 * KEY), 0) + KEY, 2 * KEY) == iota((2 * KEY, 2 * KEY), 1))
         w_all[:, :width] = w_value[...]
         w_all[:, width : width + 2 * KEY] = w_qk[...]
@@ -182,8 +186,6 @@
         pltpu.VMEM(w_class_hbm.shape, BF16),
         pltpu.VMEM((GROUPS * PAPERS, 1), jnp.int32),
     )
-    to_column(labels_ref, labels)
-
     def class_rows(m):
         main = w_mix[pl.ds(pl.multiple_of(128 * m, 128), 128), :]
         tail = w_mix[pl.ds(pl.multiple_of(tail_at + TAIL * m, TAIL), TAIL), :]
@@ -213,7 +215,7 @@
 
     def keys_to(g, h):
         return remote(
-            d_qk.at[pl.ds(2 * g, 2), part(h), :],
+            d_vq.at[pl.ds(2 * g, 2), part(h), pl.ds(width, 2 * KEY)],
             d_vk.at[:, key_rows(me, h), pl.ds(width, 2 * KEY)],
             mail_send.at[g, 2 + h],
             mail_recv.at[me, 2 + h],
@@ -224,7 +226,7 @@
         here = d_vk.at[:, key_rows(g, h), pl.ds(width, 2 * KEY)]
         return remote(here, here, mail_send.at[g, 2 + h], mail_recv.at[g, 2 + h], {"meta": g})
 
-    def head(h, carry):
+    def head(values, attention, kq, h, carry):
         for g in groups:
             for m in range(2):
                 in_copy(g, h, m).wait_recv()
@@ -261,8 +263,7 @@
         class_at = iota((HALF, 256), 1)
         exps = jnp.where(class_at < class_count, jnp.exp(logits), 0.0)
         total = jnp.sum(exps, axis=1, keepdims=True)
-        own = pl.ds(pl.multiple_of(me * PAPERS + h * HALF, HALF), HALF)
-        onehot = (labels[own, :] == class_at).astype(F32)
+        onehot = (labels[part(h), :] == class_at).astype(F32)
         loss_rows = jnp.log(total) - jnp.sum(onehot * logits, axis=1, keepdims=True)
         loss_acc[h] = jnp.zeros((8, 128), F32) + jnp.sum(loss_rows)
         dl = (seed * (exps / total - onehot)).astype(BF16)
@@ -295,69 +296,109 @@
             d_scores = (att * (d_att - mean) * scale).astype(BF16)
             swapped = kq[b]
             grad = jnp.where(first, dot(d_scores, swapped), dot_tn(d_scores, swapped))
-            d_qk[:, at, :] = grad.astype(BF16).reshape(METAS, BLOCK, 2 * KEY)
+            d_vq[:, at, width:] = grad.astype(BF16).reshape(METAS, BLOCK, 2 * KEY)
+            d_val = dot_tn(att.astype(BF16), dj)
+            d_vq[:, at, :width] = d_val.astype(BF16).reshape(METAS, BLOCK, width)
             return c
 
         lax.fori_loop(0, HALF // BLOCK, backward, 0, unroll=UNROLL)
         for g in groups:
             keys_to(g, h).start()
         for m in range(2):
-            d_vk[m, key_rows(me, h), width:] = d_qk[2 * me + m, part(h), :]
+            d_vk[m, key_rows(me, h), width:] = d_vq[2 * me + m, part(h), width:]
         return carry
 
-    lax.fori_loop(0, 2, head, 0)
+    def heads(*held):
+        lax.fori_loop(0, 2, functools.partial(head, *held), 0)
+
+    blocks = PAPERS // BLOCK
+    pl.run_scoped(
+        heads,
+        pltpu.VMEM((blocks, side, width), BF16),
+        pltpu.VMEM((blocks, side, side), F32),
+        pltpu.VMEM((blocks, side, 2 * KEY), BF16),
+    )
 
     def classes(g, carry):
         for m in range(2):
             grad = dot_tn(dlogits[:, :CLASS_PAD], joined[2 * g + m]).astype(BF16)
             for q in range(4):
+                lanes = slice(q * 128, (q + 1) * 128)
                 for p in range(2):
-                    cls[p, g, 4 * m + q] = grad[p * (CLASS_PAD // 2) : (p + 1) * (CLASS_PAD // 2), q * 128 : (q + 1) * 128]
+                    top = p * (CLASS_PAD // 2)
+                    cx[p, g, 4 * m + q] = grad[top : top + META_ROWS, lanes]
+                    cy[p, 4 * m + q, g] = grad[top + META_ROWS : top + CLASS_PAD // 2, lanes]
         return carry
 
     lax.fori_loop(0, GROUPS, classes, 0)
-    c0 = to_sibling(0, cls.at[other], cls_in)
-    c0.start()
+    c0 = [to_sibling(0, cx.at[other], cx_in), to_sibling(7, cy.at[other], cy_in)]
+    for copy in c0:
+        copy.start()
+
+    batch = GROUPS * PAPERS
+    part_rows = qv.shape[2]
+    for c in range(4):
+        cols = slice(c * 128, (c + 1) * 128)
+        grad = dot_tn(
+            hidden[:, :, cols].reshape(METAS * PAPERS, 128), d_vq[...].reshape(METAS * PAPERS, width + 2 * KEY)
+        ).astype(BF16)
+        for r in range(128 // part_rows):
+            piece = c * (128 // part_rows) + r
+            qv[piece // CHIPS, piece % CHIPS] = grad[r * part_rows : (r + 1) * part_rows]
+    q0 = to_sibling(1, qv.at[other], qv_in)
+    q0.start()
+
+    for copy in c0:
+        copy.wait_recv()
+
+    def pair_class(g, carry):
+        cx_in[g] = (cx[core, g].astype(F32) + cx_in[g].astype(F32)).astype(BF16)
+        cy_in[g] = (cy[core, g].astype(F32) + cy_in[g].astype(F32)).astype(BF16)
+        return carry
+
+    lax.fori_loop(0, GROUPS, pair_class, 0)
+    for k in chips:
+        to_chip(0, k, cy_in.at[k], cy_chip.at[chip]).start()
+    for g in groups:
+        to_group(1, g, cx_in.at[g], cx_meta.at[me]).start()
+    cx_meta[me] = cx_in[me]
+    cy_chip[chip] = cy_in[chip]
+
+    q0.wait_recv()
+
+    def pair_qv(k, carry):
+        qv_in[k] = (qv[core, k].astype(F32) + qv_in[k].astype(F32)).astype(BF16)
+        return carry
+
+    lax.fori_loop(0, CHIPS, pair_qv, 0)
+    for k in chips:
+        to_chip(2, k, qv_in.at[k], qv_chip.at[chip]).start()
+    qv_chip[chip] = qv_in[chip]
 
     for g in groups:
         for h in range(2):
             mail_from(g, h).wait_recv()
-    c0.wait_recv()
-
-    def pair_class(g, carry):
-        cls_in[g] = (cls[core, g].astype(F32) + cls_in[g].astype(F32)).astype(BF16)
-        return carry
-
-    lax.fori_loop(0, GROUPS, pair_class, 0)
-    for g in groups:
-        to_group(1, g, cls_in.at[g], cls_meta.at[me]).start()
-    cls_meta[me] = cls_in[me]
-
     tail_lane = iota((128, TAIL * METAS), 1)
     tail_row = iota((128, TAIL * METAS), 0)
     repeat = where_one((tail_row < TAIL) & (lax.rem(tail_lane, TAIL) == tail_row))
     widen = [where_one(tail_row == TAIL + METAS * j + tail_lane // TAIL) for j in range(2)]
 
-    def home_values(x_even, x_odd):
+    def home_values(q, x_even, x_odd):
         def build(j, x):
-            s = lax.rem(me + j, GROUPS)
-            main = mail_in[s, :, :128].astype(F32)
-            second = mail_in[s, :, 128:]
-            second_f = second.astype(F32)
-            tails = dot(second, repeat)
-            for q in range(2):
-                at = slice(q * PAPERS, (q + 1) * PAPERS)
-                x[at, tail_at:] = (tails * dot(second, widen[q])).astype(BF16)
+            for u in range(2):
+                s = lax.rem(2 * j + u, GROUPS)
+                at = slice(u * PAPERS, (u + 1) * PAPERS)
+                main = mail_in[s, :, :128].astype(F32)
+                second = mail_in[s, :, 128:]
+                second_f = second.astype(F32)
+                x[at, tail_at:] = (dot(second, repeat) * dot(second, widen[q])).astype(BF16)
                 for i in range(METAS):
                     lane = TAIL + METAS * q + i
                     x[at, 128 * i : 128 * (i + 1)] = (second_f[:, lane : lane + 1] * main).astype(BF16)
 
         def multiply(j, x):
-            s = lax.rem(me + j, GROUPS)
-            grads = dot(x[...], w_mix[...]).astype(BF16)
-            for q in range(2):
-                at = pl.ds(pl.multiple_of(s * PAPERS, PAPERS), PAPERS)
-                d_vk[q, at, :width] = grads[q * PAPERS : (q + 1) * PAPERS]
+            at = pl.ds(pl.multiple_of(2 * j * PAPERS, 2 * PAPERS), 2 * PAPERS)
+            d_vk[q, at, :width] = dot(x[...], w_mix[...]).astype(BF16)
 
         build(0, x_even)
 
@@ -368,25 +409,9 @@
             multiply(2 * t + 1, x_odd)
             return carry
 
-        lax.fori_loop(0, GROUPS // 2, two, 0)
+        lax.fori_loop(0, GROUPS // 4, two, 0)
 
     spread_shape = pltpu.VMEM((2 * PAPERS, METAS * CLASS_PAD), BF16)
-    pl.run_scoped(home_values, spread_shape, spread_shape)
-
-    for g in groups:
-        for h in range(2):
-            keys_from(g, h).wait_recv()
-
-    batch = GROUPS * PAPERS
-    part_rows = qv.shape[2]
-    for c in range(4):
-        cols = slice(c * 128, (c + 1) * 128)
-        grad = sum(dot_tn(outbox[m].reshape(batch, width)[:, cols], d_vk[m]) for m in range(2)).astype(BF16)
-        for r in range(128 // part_rows):
-            piece = c * (128 // part_rows) + r
-            qv[piece // CHIPS, piece % CHIPS] = grad[r * part_rows : (r + 1) * part_rows]
-    q0 = to_sibling(1, qv.at[other], qv_in)
-    q0.start()
 
     d_hidden = d_joined
 
@@ -402,13 +427,12 @@
 
     part_feat = gp.shape[3]
 
-    def project(m):
+    def project(m, p):
         back = d_hidden[GROUPS * m : GROUPS * (m + 1)].reshape(batch, width)
-        grad = dot_tn(gathered[m], back)
-        for p in range(2):
-            for k in range(CHIPS):
-                start = (p * CHIPS + k) * part_feat
-                gp[m, p, k] = grad[start : start + part_feat].astype(BF16)
+        cols = pl.ds(pl.multiple_of(p * CHIPS * part_feat, 128), CHIPS * part_feat)
+        grad = dot_tn(gathered[m, :, cols], back).astype(BF16)
+        for k in range(CHIPS):
+            gp[m, p, k] = grad[k * part_feat : (k + 1) * part_feat]
 
     def pair_proj(m):
         def one(k, carry):
@@ -441,27 +465,34 @@
             from_chip(11 + m, k, gp_all.at[m, core, k]).wait_recv()
             across(m, k).start()
 
+    g0 = [to_sibling(2 + 4 * m, gp.at[m, other], gp_in.at[m]) for m in range(2)]
+
+    def first_sum(m):
+        project(m, other)
+        g0[m].start()
+        project(m, core)
+        g0[m].wait_recv()
+        pair_proj(m)
+
+    pl.run_scoped(functools.partial(home_values, 0), spread_shape, spread_shape)
+    for g in groups:
+        for h in range(2):
+            keys_from(g, h).wait_recv()
     home_hidden(0)
-
-    q0.wait_recv()
-
-    def pair_qv(k, carry):
-        qv_in[k] = (qv[core, k].astype(F32) + qv_in[k].astype(F32)).astype(BF16)
+    first_sum(0)
+    pl.run_scoped(functools.partial(home_values, 1), spread_shape, spread_shape)
+
+    for k in chips:
+        from_chip(0, k, cy_chip.at[k]).wait_recv()
+
+    def chip_sum(g, carry):
+        cy_sum[g] = jnp.sum(cy_chip[:, g].astype(F32), axis=0).astype(BF16)
         return carry
 
-    lax.fori_loop(0, CHIPS, pair_qv, 0)
-    for k in chips:
-        to_chip(2, k, qv_in.at[k], qv_chip.at[chip]).start()
-    qv_chip[chip] = qv_in[chip]
-
-    project(0)
-    g0 = [to_sibling(2 + 4 * m, gp.at[m, other], gp_in.at[m]) for m in range(2)]
-    g0[0].start()
-    home_hidden(1)
-    g0[0].wait_recv()
-    pair_proj(0)
-    project(1)
-    g0[1].start()
+    lax.fori_loop(0, GROUPS, chip_sum, 0)
+    for g in groups:
+        to_group(15, g, cy_sum.at[g], cy_meta.at[me]).start()
+    cy_meta[me] = cy_sum[me]
 
     for k in chips:
         from_chip(2, k, qv_chip.at[k]).wait_recv()
@@ -471,41 +502,42 @@
         to_group(4, g, qv_meta.at[me], qv_meta.at[me]).start()
         to_group(5, g, loss_meta.at[me], loss_meta.at[me]).start()
 
-    g0[1].wait_recv()
-    pair_proj(1)
-
-    for g in groups:
-        from_group(1, g, cls_meta.at[g]).wait_recv()
+    home_hidden(1)
+    chip_proj(0)
+    first_sum(1)
+
+    for g in groups:
+        from_group(1, g, cx_meta.at[g]).wait_recv()
 
     def meta_sum(k, carry):
-        cls_k[k] = jnp.sum(cls_meta[:, k].astype(F32), axis=0).astype(BF16)
+        cx_sum[k] = jnp.sum(cx_meta[:, k].astype(F32), axis=0).astype(BF16)
         return carry
 
     lax.fori_loop(0, CHIPS, meta_sum, 0)
     for k in chips:
-        to_chip(3, k, cls_k.at[k], cls_chip.at[chip]).start()
-    cls_chip[chip] = cls_k[chip]
-
-    chip_proj(0)
+        to_chip(3, k, cx_sum.at[k], cx_chip.at[chip]).start()
+    cx_chip[chip] = cx_sum[chip]
 
     for g in groups:
         from_group(4, g, qv_meta.at[g]).wait_recv()
         from_group(5, g, loss_meta.at[g]).wait_recv()
+        from_group(15, g, cy_meta.at[g]).wait_recv()
     qv_all[core, chip] = jnp.sum(qv_meta[...].astype(F32), axis=0).astype(BF16)
     loss_node[core, chip] = jnp.sum(loss_meta[...], axis=0)
+    cls_all[core, chip, META_ROWS:, :] = jnp.sum(cy_meta[...].astype(F32), axis=0).astype(BF16)
     for k in chips:
         to_chip(7, k, qv_all.at[core, chip], qv_all.at[core, chip]).start()
         to_chip(8, k, loss_node.at[core, chip], loss_node.at[core, chip]).start()
 
+    pass_on(0)
+
+    for k in chips:
+        from_chip(3, k, cx_chip.at[k]).wait_recv()
+    cls_all[core, chip, :META_ROWS, :] = jnp.sum(cx_chip[...].astype(F32), axis=0).astype(BF16)
+    for k in chips:
+        to_chip(6, k, cls_all.at[core, chip], cls_all.at[core, chip]).start()
+
     chip_proj(1)
-
-    for k in chips:
-        from_chip(3, k, cls_chip.at[k]).wait_recv()
-    cls_all[core, chip] = jnp.sum(cls_chip[...].astype(F32), axis=0).astype(BF16)
-    for k in chips:
-        to_chip(6, k, cls_all.at[core, chip], cls_all.at[core, chip]).start()
-
-    pass_on(0)
 
     for k in chips:
         from_chip(6, k, cls_all.at[core, k]).wait_recv()
@@ -528,9 +560,8 @@
     remote(qv_all.at[other], qv_all.at[other], sib_send.at[4], sib_recv.at[4], sibling).wait_recv()
     remote(loss_node.at[other], loss_node.at[other], sib_send.at[5], sib_recv.at[5], sibling).wait_recv()
 
-    c0.wait_send()
     q0.wait_send()
-    for copy in g0 + finals:
+    for copy in c0 + g0 + finals:
         copy.wait_send()
     for g in groups:
         for h in range(2):
@@ -538,12 +569,14 @@
                 out_copy(g, h, m).wait_send()
             mail_to(g, h).wait_send()
             keys_to(g, h).wait_send()
-        to_group(1, g, cls_in.at[g], cls_meta.at[me]).wait_send()
+        to_group(1, g, cx_in.at[g], cx_meta.at[me]).wait_send()
+        to_group(15, g, cy_sum.at[g], cy_meta.at[me]).wait_send()
         to_group(4, g, qv_meta.at[me], qv_meta.at[me]).wait_send()
         to_group(5, g, loss_meta.at[me], loss_meta.at[me]).wait_send()
     for k in chips:
         to_chip(2, k, qv_in.at[k], qv_chip.at[chip]).wait_send()
-        to_chip(3, k, cls_k.at[k], cls_chip.at[chip]).wait_send()
+        to_chip(0, k, cy_in.at[k], cy_chip.at[chip]).wait_send()
+        to_chip(3, k, cx_sum.at[k], cx_chip.at[chip]).wait_send()
         to_chip(6, k, cls_all.at[core, chip], cls_all.at[core, chip]).wait_send()
         to_chip(7, k, qv_all.at[core, chip], qv_all.at[core, chip]).wait_send()
         to_chip(8, k, loss_node.at[core, chip], loss_node.at[core, chip]).wait_send()
@@ -602,7 +635,6 @@
     batch = batch_ids.shape[0]
     width = w_value.shape[0]
     side = BLOCK * METAS
-    blocks = PAPERS // BLOCK
     mixed = width + 2 * KEY
     half = CLASS_PAD // 2
     part = feat // (2 * CHIPS)
@@ -621,7 +653,7 @@
         out_specs=(vmem,) * 4,
         scratch_shapes=[
             pltpu.SemaphoreType.DMA((10,)),
-            pltpu.VMEM((batch, 1), jnp.int32),
+            pltpu.VMEM((PAPERS, 1), jnp.int32),
             pltpu.VMEM((count, batch, feat), BF16),
             pltpu.VMEM((count, GROUPS, PAPERS, width), BF16),
             pltpu.VMEM((METAS, PAPERS, width), BF16),
@@ -630,20 +662,22 @@
             pltpu.VMEM((METAS * CLASS_PAD, width), BF16),
             pltpu.VMEM((METAS, PAPERS, width), BF16),
             pltpu.VMEM((METAS, PAPERS, width), BF16),
-            pltpu.VMEM((blocks, side, width), BF16),
-            pltpu.VMEM((blocks, side, side), F32),
-            pltpu.VMEM((blocks, side, 2 * KEY), BF16),
             pltpu.VMEM((PAPERS, 256), BF16),
             pltpu.VMEM((PAPERS, side), BF16),
             pltpu.VMEM((GROUPS, PAPERS, 256), BF16),
             pltpu.VMEM((GROUPS, PAPERS, 256), BF16),
-            pltpu.VMEM((METAS, PAPERS, 2 * KEY), BF16),
+            pltpu.VMEM((METAS, PAPERS, mixed), BF16),
             pltpu.VMEM((count, batch, mixed), BF16),
-            pltpu.VMEM((2, GROUPS, CHIPS, half, 128), BF16),
-            pltpu.VMEM((GROUPS, CHIPS, half, 128), BF16),
-            pltpu.VMEM((GROUPS, CHIPS, half, 128), BF16),
-            pltpu.VMEM((CHIPS, half, 128), BF16),
-            pltpu.VMEM((CHIPS, half, 128), BF16),
+            pltpu.VMEM((2, GROUPS, CHIPS, META_ROWS, 128), BF16),
+            pltpu.VMEM((GROUPS, CHIPS, META_ROWS, 128), BF16),
+            pltpu.VMEM((GROUPS, CHIPS, META_ROWS, 128), BF16),
+            pltpu.VMEM((CHIPS, META_ROWS, 128), BF16),
+            pltpu.VMEM((CHIPS, META_ROWS, 128), BF16),
+            pltpu.VMEM((2, CHIPS, GROUPS, half - META_ROWS, 128), BF16),
+            pltpu.VMEM((CHIPS, GROUPS, half - META_ROWS, 128), BF16),
+            pltpu.VMEM((CHIPS, GROUPS, half - META_ROWS, 128), BF16),
+            pltpu.VMEM((GROUPS, half - META_ROWS, 128), BF16),
+            pltpu.VMEM((GROUPS, half - META_ROWS, 128), BF16),
             pltpu.VMEM((2, CHIPS, part_rows, mixed), BF16),
             pltpu.VMEM((CHIPS, part_rows, mixed), BF16),
             pltpu.VMEM((CHIPS, part_rows, mixed), BF16),
@@ -657,10 +691,10 @@
             pltpu.SemaphoreType.DMA((GROUPS, 4)),
             pltpu.SemaphoreType.DMA((GROUPS, 4)),
             pltpu.SemaphoreType.DMA((GROUPS, 4)),
-            pltpu.SemaphoreType.DMA((15, 8)),
-            pltpu.SemaphoreType.DMA((15, 8)),
-            pltpu.SemaphoreType.DMA((7,)),
-            pltpu.SemaphoreType.DMA((7,)),
+            pltpu.SemaphoreType.DMA((16, 8)),
+            pltpu.SemaphoreType.DMA((16, 8)),
+            pltpu.SemaphoreType.DMA((8,)),
+            pltpu.SemaphoreType.DMA((8,)),
         ],
         compiler_params=pltpu.CompilerParams(
             collective_id=1, has_side_effects=True, vmem_limit_bytes=62 * 1024 * 1024
@@ -688,7 +722,7 @@
             pltpu.SemaphoreType.DMA((5,)),
             pltpu.SemaphoreType.DMA((2,)),
         ],
-        compiler_params=pltpu.CompilerParams(vmem_limit_bytes=32 * 1024 * 1024),
+        compiler_params=pltpu.CompilerParams(vmem_limit_bytes=62 * 1024 * 1024),
     )(*sums)
     return (grad_proj, grad_qk, grad_value, grad_class, loss.reshape(()))
 

time: 145 us -> 133 us (0.917)
  Pallas kernels: 139 us -> 132 us
  local copies, waits for them, and re-layouts: 4.3 us -> 0 us
    pallas_call x1, Pallas kernels: 135 us -> 128 us  [local(): pl.pallas_call(functools.partial(step_kernel, 1.0 / batch_total ** 0.5, c...]
    unnamed x8 -> x0, local copies, waits for them, and re-layouts: 4.3 us -> none
where the time goes in v4:
time: 133 us
  Pallas kernels  132 us (99%)
    pallas_call x1, Pallas kernels, local(): pl.pallas_call(functools.partial(step_kernel, 1.0 / batch_total ** 0.5, c...  128 us
    pallas_call x1, Pallas kernels, local(): pl.pallas_call(functools.partial(finish_kernel, batch_total, class_count)...  4.23 us

profile of v4, /device:TPU:1, one launch (start us, length us, event | category | flops | bytes accessed | tf_op | source)
XLA Modules:
  0.0 133.2 jit_solution(3083340441337136550)
XLA Ops:
  0.6 128.2 %shard_map.110 = (bf16[2,2,8,48,512]{4,3,2,1,0:T(8,128)(2,1)}, bf16[2,8,80,128]{3,2,1,0:T(8,128)(2,1)}, bf16[2,8,32,640]{3,2,1,0:T(8,128)(2,1)}, f32[2,8,8,128]{3,2,1,0:T(8,128)}) custom-call(s32[12,128]{1,0:T(8,128)} %bitcast.3, s32[12,128]{1,0:T(8,128)} %bitcast.4, bf16[2,2048,768]{2,1,0:T(8,128)(2,1)} %agg_hbm.1, bf16[2,768,512]{2,1,0:T(8,128)(2,1)} %w_proj_hbm.1, ...), custom_call_target="tpu_custom_call" | custom-call | tf_op jit(solution)/shard_map/pallas_call | solution.py:644
  128.8 4.2 %shard_map.111 = (f32[2,768,512]{2,1,0:T(8,128)}, f32[512,128]{1,0:T(8,128)}, f32[512,512]{1,0:T(8,128)}, f32[153,1024]{1,0:T(8,128)}, f32[1,1]{1,0:T(1,128)}) custom-call(bf16[2,2,8,48,512]{4,3,2,1,0:T(8,128)(2,1)} %get-tuple-element.14.gp_hbm, bf16[2,8,80,128]{3,2,1,0:T(8,128)(2,1)} %get-tuple-element.15.cls_hbm, ...), custom_call_target="tpu_custom_call" | custom-call | tf_op jit(solution)/shard_map/pallas_call | solution.py:705

commit v5 on v4

--- a/solution.py
+++ b/solution.py
@@ -51,13 +51,12 @@
 
 def step_kernel(
     seed, class_count,
-    ids_ref, labels_ref, agg_hbm, w_proj_hbm, w_qk, w_value, w_class_hbm,
-    gp_all, cls_all, qv_all, loss_node,
+    ids_ref, labels_hbm, agg_hbm, w_proj_hbm, w_qk_hbm, w_value_hbm, w_class_hbm,
+    gp_all, fin,
     load_sem, labels, gathered, outbox, hidden, w_all, w_back, w_mix,
     joined, d_joined, dlogits, attended, mail, mail_in, d_vq, d_vk,
-    cx, cx_in, cx_meta, cx_sum, cx_chip, cy, cy_in, cy_chip, cy_sum, cy_meta,
-    qv, qv_in, qv_chip, qv_meta,
-    gp, gp_in, gp_chip, loss_acc, loss_meta,
+    sx, sx_in, sx_meta, sx_sum, sx_chip, sy, sy_in, sy_chip, sy_sum, sy_meta,
+    gp, gp_in, gp_chip, loss_acc,
     out_sem, in_sem, mail_send, mail_recv, send_sem, recv_sem, sib_send, sib_recv,
 ):
     me = lax.axis_index("meta")
@@ -67,7 +66,7 @@
     sibling = {"node": 2 * chip + other}
     groups = [lax.rem(me + j, GROUPS) for j in range(1, GROUPS)]
     chips = [lax.rem(chip + j, CHIPS) for j in range(1, CHIPS)]
-    width = w_value.shape[0]
+    width = w_value_hbm.shape[0]
     rows, feat = agg_hbm.shape[1:]
     tail_at = 128 * METAS
 
@@ -115,21 +114,23 @@
         here = hidden.at[2 * g + m, part(h), :]
         return remote(here, here, out_sem.at[g, 2 * h + m], in_sem.at[g, 2 * h + m], {"meta": g})
 
-    def front(agg, w_proj, w_class, ids):
+    def front(agg, w_proj, w_class, ids, labels_ref, w_qk, w_value):
         loads = []
         step = rows // 4
         for m in range(2):
             for q in range(4):
                 at = pl.ds(q * step, step)
                 loads.append(pltpu.make_async_copy(agg_hbm.at[m, at, :], agg.at[m, at, :], load_sem.at[4 * m + q]))
-        loads.append(pltpu.make_async_copy(w_proj_hbm, w_proj, load_sem.at[8]))
-        loads.append(pltpu.make_async_copy(w_class_hbm, w_class, load_sem.at[9]))
-        for load in loads:
+            loads.append(pltpu.make_async_copy(w_proj_hbm.at[m], w_proj.at[m], load_sem.at[8 + m]))
+        later = [
+            pltpu.make_async_copy(src, dst, load_sem.at[10 + q])
+            for q, (src, dst) in enumerate(
+                ((w_class_hbm, w_class), (labels_hbm, labels_ref), (w_qk_hbm, w_qk), (w_value_hbm, w_value))
+            )
+        ]
+        for load in loads + later:
             load.start()
         to_column(ids_ref, ids)
-        for load in loads[:9]:
-            load.wait()
-        pl.semaphore_wait(barrier, GROUPS - 1 + CHIPS)
 
         def project_pair(p, h, with_own):
             first = lax.rem(me // 2 + p + 1, 4) * 2 + lax.rem(me + p, 2)
@@ -140,8 +141,21 @@
             column = jnp.concatenate([ids[spot, :] for spot in spots], axis=0)
             picks = where_one(column == iota((2 * HALF, rows), 1))
             for m in range(2):
+                if not with_own:
+
+                    @pl.when(h + p == 0)
+                    def _():
+                        for load in loads[5 * m : 5 * m + 5]:
+                            load.wait()
+
                 got = dot(picks, agg[m]).astype(BF16)
                 row = dot(got, w_proj[m]).astype(BF16)
+                if m == 0 and not with_own:
+
+                    @pl.when(h + p == 0)
+                    def _():
+                        pl.semaphore_wait(barrier, GROUPS - 1 + CHIPS)
+
                 for q, g in enumerate((first, second)):
                     gathered[m, spots[q], :] = got[q * HALF : (q + 1) * HALF]
                     mine = row[q * HALF : (q + 1) * HALF]
@@ -162,6 +176,8 @@
 
         lax.fori_loop(0, 2, project_half, 0)
 
+        for load in later:
+            load.wait()
         to_column(labels_ref, ids)
         labels[...] = ids[pl.ds(pl.multiple_of(me * PAPERS, PAPERS), PAPERS), :]
 
@@ -171,7 +187,6 @@
         w_all[:, width + 2 * KEY :] = dot(w_qk[...], swap).astype(BF16)
         w_back[:width, :] = w_value[...].astype(F32).T.astype(BF16)
         w_back[width:, :] = w_qk[...].astype(F32).T.astype(BF16)
-        loads[9].wait()
         for m in range(METAS):
             lanes = slice(m * width, (m + 1) * width)
             w_mix[128 * m : 128 * (m + 1), :] = w_class[:128, lanes]
@@ -185,6 +200,9 @@
         pltpu.VMEM(w_proj_hbm.shape, BF16),
         pltpu.VMEM(w_class_hbm.shape, BF16),
         pltpu.VMEM((GROUPS * PAPERS, 1), jnp.int32),
+        pltpu.VMEM(labels_hbm.shape, jnp.int32),
+        pltpu.VMEM(w_qk_hbm.shape, BF16),
+        pltpu.VMEM(w_value_hbm.shape, BF16),
     )
     def class_rows(m):
         main = w_mix[pl.ds(pl.multiple_of(128 * m, 128), 128), :]
@@ -209,22 +227,6 @@
     def mail_from(g, h):
         here = mail_in.at[g, part(h), :]
         return remote(here, here, mail_send.at[g, h], mail_recv.at[g, h], {"meta": g})
-
-    def key_rows(g, h):
-        return pl.ds(pl.multiple_of(g * PAPERS + h * HALF, HALF), HALF)
-
-    def keys_to(g, h):
-        return remote(
-            d_vq.at[pl.ds(2 * g, 2), part(h), pl.ds(width, 2 * KEY)],
-            d_vk.at[:, key_rows(me, h), pl.ds(width, 2 * KEY)],
-            mail_send.at[g, 2 + h],
-            mail_recv.at[me, 2 + h],
-            {"meta": g},
-        )
-
-    def keys_from(g, h):
-        here = d_vk.at[:, key_rows(g, h), pl.ds(width, 2 * KEY)]
-        return remote(here, here, mail_send.at[g, 2 + h], mail_recv.at[g, 2 + h], {"meta": g})
 
     def head(values, attention, kq, h, carry):
         for g in groups:
@@ -276,9 +278,7 @@
             second = (dl[:, 128:].astype(F32) + dot(attended[part(h), :], choose)).astype(BF16)
             box = mail_in if j == 0 else mail
             box[g, part(h), :128] = dl[:, :128]
-            box[g, part(h), 128:] = second
-            if j:
-                mail_to(g, h).start()
+            box[g, part(h), 128:256] = second
 
         def spread(m, c):
             d_joined[m, part(h), :] = dot(dl[:, :CLASS_PAD], class_rows(m)).astype(BF16)
@@ -302,10 +302,14 @@
             return c
 
         lax.fori_loop(0, HALF // BLOCK, backward, 0, unroll=UNROLL)
-        for g in groups:
-            keys_to(g, h).start()
-        for m in range(2):
-            d_vk[m, key_rows(me, h), width:] = d_vq[2 * me + m, part(h), width:]
+        for j in range(GROUPS):
+            g = lax.rem(me + j, GROUPS)
+            box = mail_in if j == 0 else mail
+            for m in range(2):
+                lanes = slice(256 + 2 * KEY * m, 256 + 2 * KEY * (m + 1))
+                box[g, part(h), lanes] = d_vq[2 * g + m, part(h), width:]
+            if j:
+                mail_to(g, h).start()
         return carry
 
     def heads(*held):
@@ -319,61 +323,63 @@
         pltpu.VMEM((blocks, side, 2 * KEY), BF16),
     )
 
+    node_rows = CLASS_PAD // 2 - META_ROWS
+    loss_part = loss_acc[0][:1, :1] + loss_acc[1][:1, :1]
+
     def classes(g, carry):
         for m in range(2):
-            grad = dot_tn(dlogits[:, :CLASS_PAD], joined[2 * g + m]).astype(BF16)
+            grad = dot_tn(dlogits[:, :CLASS_PAD], joined[2 * g + m])
+            grad = jnp.where(iota((CLASS_PAD, width), 0) == class_count, loss_part, grad).astype(BF16)
             for q in range(4):
                 lanes = slice(q * 128, (q + 1) * 128)
                 for p in range(2):
                     top = p * (CLASS_PAD // 2)
-                    cx[p, g, 4 * m + q] = grad[top : top + META_ROWS, lanes]
-                    cy[p, 4 * m + q, g] = grad[top + META_ROWS : top + CLASS_PAD // 2, lanes]
+                    sx[p, g, 4 * m + q] = grad[top : top + META_ROWS, lanes]
+                    sy[p, 4 * m + q, pl.ds(pl.multiple_of(g * node_rows, node_rows), node_rows), :] = grad[top + META_ROWS : top + CLASS_PAD // 2, lanes]
         return carry
 
     lax.fori_loop(0, GROUPS, classes, 0)
-    c0 = [to_sibling(0, cx.at[other], cx_in), to_sibling(7, cy.at[other], cy_in)]
-    for copy in c0:
-        copy.start()
+    c0 = [to_sibling(0, sx.at[other], sx_in), to_sibling(1, sy.at[other], sy_in)]
+    c0[0].start()
 
     batch = GROUPS * PAPERS
-    part_rows = qv.shape[2]
+    qv_at = GROUPS * node_rows
+    qv_rows = width // (2 * CHIPS)
+    tiles = (width + 2 * KEY) // 128
     for c in range(4):
         cols = slice(c * 128, (c + 1) * 128)
         grad = dot_tn(
             hidden[:, :, cols].reshape(METAS * PAPERS, 128), d_vq[...].reshape(METAS * PAPERS, width + 2 * KEY)
         ).astype(BF16)
-        for r in range(128 // part_rows):
-            piece = c * (128 // part_rows) + r
-            qv[piece // CHIPS, piece % CHIPS] = grad[r * part_rows : (r + 1) * part_rows]
-    q0 = to_sibling(1, qv.at[other], qv_in)
-    q0.start()
-
-    for copy in c0:
-        copy.wait_recv()
-
-    def pair_class(g, carry):
-        cx_in[g] = (cx[core, g].astype(F32) + cx_in[g].astype(F32)).astype(BF16)
-        cy_in[g] = (cy[core, g].astype(F32) + cy_in[g].astype(F32)).astype(BF16)
+        for r in range(128 // qv_rows):
+            piece = c * (128 // qv_rows) + r
+            for t in range(tiles):
+                sy[piece // CHIPS, piece % CHIPS, qv_at + t * qv_rows : qv_at + (t + 1) * qv_rows, :] = grad[
+                    r * qv_rows : (r + 1) * qv_rows, t * 128 : (t + 1) * 128
+                ]
+    c0[1].start()
+
+    c0[0].wait_recv()
+
+    def pair_x(g, carry):
+        sx_in[g] = (sx[core, g].astype(F32) + sx_in[g].astype(F32)).astype(BF16)
         return carry
 
-    lax.fori_loop(0, GROUPS, pair_class, 0)
+    lax.fori_loop(0, GROUPS, pair_x, 0)
+    for g in groups:
+        to_group(1, g, sx_in.at[g], sx_meta.at[me]).start()
+    sx_meta[me] = sx_in[me]
+
+    c0[1].wait_recv()
+
+    def pair_y(k, carry):
+        sy_in[k] = (sy[core, k].astype(F32) + sy_in[k].astype(F32)).astype(BF16)
+        return carry
+
+    lax.fori_loop(0, CHIPS, pair_y, 0)
     for k in chips:
-        to_chip(0, k, cy_in.at[k], cy_chip.at[chip]).start()
-    for g in groups:
-        to_group(1, g, cx_in.at[g], cx_meta.at[me]).start()
-    cx_meta[me] = cx_in[me]
-    cy_chip[chip] = cy_in[chip]
-
-    q0.wait_recv()
-
-    def pair_qv(k, carry):
-        qv_in[k] = (qv[core, k].astype(F32) + qv_in[k].astype(F32)).astype(BF16)
-        return carry
-
-    lax.fori_loop(0, CHIPS, pair_qv, 0)
-    for k in chips:
-        to_chip(2, k, qv_in.at[k], qv_chip.at[chip]).start()
-    qv_chip[chip] = qv_in[chip]
+        to_chip(2, k, sy_in.at[k], sy_chip.at[chip]).start()
+    sy_chip[chip] = sy_in[chip]
 
     for g in groups:
         for h in range(2):
@@ -389,7 +395,7 @@
                 s = lax.rem(2 * j + u, GROUPS)
                 at = slice(u * PAPERS, (u + 1) * PAPERS)
                 main = mail_in[s, :, :128].astype(F32)
-                second = mail_in[s, :, 128:]
+                second = mail_in[s, :, 128:256]
                 second_f = second.astype(F32)
                 x[at, tail_at:] = (dot(second, repeat) * dot(second, widen[q])).astype(BF16)
                 for i in range(METAS):
@@ -398,7 +404,7 @@
 
         def multiply(j, x):
             at = pl.ds(pl.multiple_of(2 * j * PAPERS, 2 * PAPERS), 2 * PAPERS)
-            d_vk[q, at, :width] = dot(x[...], w_mix[...]).astype(BF16)
+            d_vk[q, at, :] = dot(x[...], w_mix[...]).astype(BF16)
 
         build(0, x_even)
 
@@ -418,8 +424,10 @@
     def home_hidden(m):
         def some(r, carry):
             at = pl.ds(pl.multiple_of(r * 2 * PAPERS, 2 * PAPERS), 2 * PAPERS)
-            letters = mail_in[pl.ds(2 * r, 2)].reshape(2 * PAPERS, 256)[:, :CLASS_PAD]
-            grad = dot(letters, class_rows(2 * me + m)) + dot(d_vk[m, at, :], w_back[...])
+            letters = mail_in[pl.ds(2 * r, 2)].reshape(2 * PAPERS, 512)
+            keys = letters[:, 256 + 2 * KEY * m : 256 + 2 * KEY * (m + 1)]
+            both = jnp.concatenate([d_vk[m, at, :], keys], axis=1)
+            grad = dot(letters[:, :CLASS_PAD], class_rows(2 * me + m)) + dot(both, w_back[...])
             d_hidden[pl.ds(GROUPS * m + 2 * r, 2)] = grad.astype(BF16).reshape(2, PAPERS, width)
             return carry
 
@@ -444,13 +452,12 @@
             to_chip(9 + m, k, gp_in.at[m, k], gp_chip.at[m, chip]).start()
         gp_chip[m, chip] = gp_in[m, chip]
 
-    def across(m, k):
-        here = gp_all.at[m, core, k]
-        return remote(here, here, send_sem.at[13 + m, k], recv_sem.at[13 + m, k], sibling)
-
-    def across_in(m, k):
-        here = gp_all.at[m, other, k]
-        return remote(here, here, send_sem.at[13 + m, k], recv_sem.at[13 + m, k], sibling)
+    def across(m):
+        return to_sibling(3 + m, gp_all.at[m, core], gp_all.at[m, core])
+
+    def across_in(m):
+        here = gp_all.at[m, other]
+        return remote(here, here, sib_send.at[3 + m], sib_recv.at[3 + m], sibling)
 
     def chip_proj(m):
         for k in chips:
@@ -458,14 +465,13 @@
         gp_all[m, core, chip] = jnp.sum(gp_chip[m].astype(F32), axis=0).astype(BF16)
         for k in chips:
             to_chip(11 + m, k, gp_all.at[m, core, chip], gp_all.at[m, core, chip]).start()
-        across(m, chip).start()
 
     def pass_on(m):
         for k in chips:
             from_chip(11 + m, k, gp_all.at[m, core, k]).wait_recv()
-            across(m, k).start()
-
-    g0 = [to_sibling(2 + 4 * m, gp.at[m, other], gp_in.at[m]) for m in range(2)]
+        across(m).start()
+
+    g0 = [to_sibling(5 + m, gp.at[m, other], gp_in.at[m]) for m in range(2)]
 
     def first_sum(m):
         project(m, other)
@@ -475,130 +481,98 @@
         pair_proj(m)
 
     pl.run_scoped(functools.partial(home_values, 0), spread_shape, spread_shape)
-    for g in groups:
-        for h in range(2):
-            keys_from(g, h).wait_recv()
     home_hidden(0)
     first_sum(0)
+
+    for k in chips:
+        from_chip(2, k, sy_chip.at[k]).wait_recv()
+    qv_sum = jnp.sum(sy_chip[:, qv_at:, :].astype(F32), axis=0).astype(BF16)
+
+    def chip_sum(g, carry):
+        at = pl.ds(pl.multiple_of(g * node_rows, node_rows), node_rows)
+        sy_sum[g, :node_rows, :] = jnp.sum(sy_chip[:, at, :].astype(F32), axis=0).astype(BF16)
+        return carry
+
+    lax.fori_loop(0, GROUPS, chip_sum, 0)
+    for g in range(GROUPS):
+        sy_sum[g, node_rows:, :] = qv_sum
+    for g in groups:
+        to_group(3, g, sy_sum.at[g], sy_meta.at[me]).start()
+    sy_meta[me] = sy_sum[me]
+
     pl.run_scoped(functools.partial(home_values, 1), spread_shape, spread_shape)
 
+    for g in groups:
+        from_group(1, g, sx_meta.at[g]).wait_recv()
+
+    def meta_sum(k, carry):
+        sx_sum[k] = jnp.sum(sx_meta[:, k].astype(F32), axis=0).astype(BF16)
+        return carry
+
+    lax.fori_loop(0, CHIPS, meta_sum, 0)
     for k in chips:
-        from_chip(0, k, cy_chip.at[k]).wait_recv()
-
-    def chip_sum(g, carry):
-        cy_sum[g] = jnp.sum(cy_chip[:, g].astype(F32), axis=0).astype(BF16)
-        return carry
-
-    lax.fori_loop(0, GROUPS, chip_sum, 0)
-    for g in groups:
-        to_group(15, g, cy_sum.at[g], cy_meta.at[me]).start()
-    cy_meta[me] = cy_sum[me]
-
-    for k in chips:
-        from_chip(2, k, qv_chip.at[k]).wait_recv()
-    qv_meta[me] = jnp.sum(qv_chip[...].astype(F32), axis=0).astype(BF16)
-    loss_meta[me] = loss_acc[0] + loss_acc[1]
-    for g in groups:
-        to_group(4, g, qv_meta.at[me], qv_meta.at[me]).start()
-        to_group(5, g, loss_meta.at[me], loss_meta.at[me]).start()
+        to_chip(4, k, sx_sum.at[k], sx_chip.at[chip]).start()
+    sx_chip[chip] = sx_sum[chip]
 
     home_hidden(1)
     chip_proj(0)
     first_sum(1)
 
     for g in groups:
-        from_group(1, g, cx_meta.at[g]).wait_recv()
-
-    def meta_sum(k, carry):
-        cx_sum[k] = jnp.sum(cx_meta[:, k].astype(F32), axis=0).astype(BF16)
-        return carry
-
-    lax.fori_loop(0, CHIPS, meta_sum, 0)
+        from_group(3, g, sy_meta.at[g]).wait_recv()
+    fin[core, chip, META_ROWS:, :] = jnp.sum(sy_meta[...].astype(F32), axis=0).astype(BF16)
     for k in chips:
-        to_chip(3, k, cx_sum.at[k], cx_chip.at[chip]).start()
-    cx_chip[chip] = cx_sum[chip]
-
-    for g in groups:
-        from_group(4, g, qv_meta.at[g]).wait_recv()
-        from_group(5, g, loss_meta.at[g]).wait_recv()
-        from_group(15, g, cy_meta.at[g]).wait_recv()
-    qv_all[core, chip] = jnp.sum(qv_meta[...].astype(F32), axis=0).astype(BF16)
-    loss_node[core, chip] = jnp.sum(loss_meta[...], axis=0)
-    cls_all[core, chip, META_ROWS:, :] = jnp.sum(cy_meta[...].astype(F32), axis=0).astype(BF16)
+        from_chip(4, k, sx_chip.at[k]).wait_recv()
+    fin[core, chip, :META_ROWS, :] = jnp.sum(sx_chip[...].astype(F32), axis=0).astype(BF16)
     for k in chips:
-        to_chip(7, k, qv_all.at[core, chip], qv_all.at[core, chip]).start()
-        to_chip(8, k, loss_node.at[core, chip], loss_node.at[core, chip]).start()
+        to_chip(6, k, fin.at[core, chip], fin.at[core, chip]).start()
 
     pass_on(0)
 
+    chip_proj(1)
+
     for k in chips:
-        from_chip(3, k, cx_chip.at[k]).wait_recv()
-    cls_all[core, chip, :META_ROWS, :] = jnp.sum(cx_chip[...].astype(F32), axis=0).astype(BF16)
-    for k in chips:
-        to_chip(6, k, cls_all.at[core, chip], cls_all.at[core, chip]).start()
-
-    chip_proj(1)
-
-    for k in chips:
-        from_chip(6, k, cls_all.at[core, k]).wait_recv()
-        from_chip(7, k, qv_all.at[core, k]).wait_recv()
-        from_chip(8, k, loss_node.at[core, k]).wait_recv()
-    finals = [
-        to_sibling(3, cls_all.at[core], cls_all.at[core]),
-        to_sibling(4, qv_all.at[core], qv_all.at[core]),
-        to_sibling(5, loss_node.at[core], loss_node.at[core]),
-    ]
-    for copy in finals:
-        copy.start()
+        from_chip(6, k, fin.at[core, k]).wait_recv()
+    last = to_sibling(2, fin.at[core], fin.at[core])
+    last.start()
 
     pass_on(1)
 
     for m in range(2):
-        for k in [chip] + chips:
-            across_in(m, k).wait_recv()
-    remote(cls_all.at[other], cls_all.at[other], sib_send.at[3], sib_recv.at[3], sibling).wait_recv()
-    remote(qv_all.at[other], qv_all.at[other], sib_send.at[4], sib_recv.at[4], sibling).wait_recv()
-    remote(loss_node.at[other], loss_node.at[other], sib_send.at[5], sib_recv.at[5], sibling).wait_recv()
-
-    q0.wait_send()
-    for copy in c0 + g0 + finals:
+        across_in(m).wait_recv()
+    remote(fin.at[other], fin.at[other], sib_send.at[2], sib_recv.at[2], sibling).wait_recv()
+
+    last.wait_send()
+    for copy in c0 + g0:
         copy.wait_send()
     for g in groups:
         for h in range(2):
             for m in range(2):
                 out_copy(g, h, m).wait_send()
             mail_to(g, h).wait_send()
-            keys_to(g, h).wait_send()
-        to_group(1, g, cx_in.at[g], cx_meta.at[me]).wait_send()
-        to_group(15, g, cy_sum.at[g], cy_meta.at[me]).wait_send()
-        to_group(4, g, qv_meta.at[me], qv_meta.at[me]).wait_send()
-        to_group(5, g, loss_meta.at[me], loss_meta.at[me]).wait_send()
+        to_group(1, g, sx_in.at[g], sx_meta.at[me]).wait_send()
+        to_group(3, g, sy_sum.at[g], sy_meta.at[me]).wait_send()
     for k in chips:
-        to_chip(2, k, qv_in.at[k], qv_chip.at[chip]).wait_send()
-        to_chip(0, k, cy_in.at[k], cy_chip.at[chip]).wait_send()
-        to_chip(3, k, cx_sum.at[k], cx_chip.at[chip]).wait_send()
-        to_chip(6, k, cls_all.at[core, chip], cls_all.at[core, chip]).wait_send()
-        to_chip(7, k, qv_all.at[core, chip], qv_all.at[core, chip]).wait_send()
-        to_chip(8, k, loss_node.at[core, chip], loss_node.at[core, chip]).wait_send()
+        to_chip(2, k, sy_in.at[k], sy_chip.at[chip]).wait_send()
+        to_chip(4, k, sx_sum.at[k], sx_chip.at[chip]).wait_send()
+        to_chip(6, k, fin.at[core, chip], fin.at[core, chip]).wait_send()
     for m in range(2):
         for k in chips:
             to_chip(9 + m, k, gp_in.at[m, k], gp_chip.at[m, chip]).wait_send()
             to_chip(11 + m, k, gp_all.at[m, core, chip], gp_all.at[m, core, chip]).wait_send()
-        for k in [chip] + chips:
-            across(m, k).wait_send()
+        across(m).wait_send()
 
 
 def finish_kernel(
     batch_total, class_count,
-    gp_hbm, cls_hbm, qv_hbm, loss_hbm, proj_hbm, qk_out, value_out, class_out, loss_out,
-    gp, cls, qv, loss, proj, in_sem, out_sem,
+    gp_hbm, fin_hbm, proj_hbm, qk_out, value_out, class_out, loss_out,
+    gp, fin, proj, in_sem, out_sem,
 ):
     part_feat, width = gp.shape[3:]
-    part_rows = qv.shape[2]
-    half_rows = cls.shape[2]
+    qv_rows = width // (2 * CHIPS)
+    half_rows = CLASS_PAD // 2
     loads = [pltpu.make_async_copy(gp_hbm.at[m], gp.at[m], in_sem.at[m]) for m in range(2)]
-    for q, (src, dst) in enumerate(((cls_hbm, cls), (qv_hbm, qv), (loss_hbm, loss))):
-        loads.append(pltpu.make_async_copy(src, dst, in_sem.at[2 + q]))
+    loads.append(pltpu.make_async_copy(fin_hbm, fin, in_sem.at[2]))
     for load in loads:
         load.start()
     stores = []
@@ -610,20 +584,24 @@
                 proj[m, start : start + part_feat, :] = gp[m, p, k].astype(F32)
         stores.append(pltpu.make_async_copy(proj.at[m], proj_hbm.at[m], out_sem.at[m]))
         stores[m].start()
-    for load in loads[2:]:
-        load.wait()
+    loads[2].wait()
+    left = class_count - half_rows
     for p in range(2):
         for k in range(CHIPS):
-            start = (p * CHIPS + k) * part_rows
-            block = qv[p, k].astype(F32)
-            value_out[start : start + part_rows, :] = block[:, :width]
-            qk_out[start : start + part_rows, :] = block[:, width:]
+            start = (p * CHIPS + k) * qv_rows
+            for t in range(width // 128 + 1):
+                block = fin[p, k, half_rows + t * qv_rows : half_rows + (t + 1) * qv_rows, :].astype(F32)
+                if t < width // 128:
+                    value_out[start : start + qv_rows, t * 128 : (t + 1) * 128] = block
+                else:
+                    qk_out[start : start + qv_rows, :] = block
             lanes = slice(k * 128, (k + 1) * 128)
+            block = fin[p, k, :half_rows, :].astype(F32)
             if p == 0:
-                class_out[:half_rows, lanes] = cls[0, k].astype(F32)
+                class_out[:half_rows, lanes] = block
             else:
-                class_out[half_rows:, lanes] = cls[1, k].astype(F32)[: class_count - half_rows]
-    loss_out[0, 0] = jnp.sum(loss[...].reshape(2 * CHIPS, 8, 128), axis=0)[0, 0] / batch_total
+                class_out[half_rows:, lanes] = block[:left]
+    loss_out[0, 0] = fin[1, 0, :half_rows, :].astype(F32)[left, 0] / batch_total
     for store in stores:
         store.wait()
 
@@ -638,21 +616,21 @@
     mixed = width + 2 * KEY
     half = CLASS_PAD // 2
     part = feat // (2 * CHIPS)
-    part_rows = width // (2 * CHIPS)
+    node_rows = half - META_ROWS
+    qv_rows = width // (2 * CHIPS) * (mixed // 128)
+    fin_rows = half + qv_rows
     vmem = pl.BlockSpec(memory_space=pltpu.VMEM)
     anywhere = pl.BlockSpec(memory_space=pl.ANY)
     sums = pl.pallas_call(
         functools.partial(step_kernel, 1.0 / batch_total**0.5, class_count),
         out_shape=(
             jax.ShapeDtypeStruct((count, 2, CHIPS, part, width), BF16),
-            jax.ShapeDtypeStruct((2, CHIPS, half, 128), BF16),
-            jax.ShapeDtypeStruct((2, CHIPS, part_rows, mixed), BF16),
-            jax.ShapeDtypeStruct((2, CHIPS, 8, 128), F32),
+            jax.ShapeDtypeStruct((2, CHIPS, fin_rows, 128), BF16),
         ),
-        in_specs=[vmem, vmem, anywhere, anywhere, vmem, vmem, anywhere],
-        out_specs=(vmem,) * 4,
+        in_specs=[vmem] + [anywhere] * 6,
+        out_specs=(vmem,) * 2,
         scratch_shapes=[
-            pltpu.SemaphoreType.DMA((10,)),
+            pltpu.SemaphoreType.DMA((14,)),
             pltpu.VMEM((PAPERS, 1), jnp.int32),
             pltpu.VMEM((count, batch, feat), BF16),
             pltpu.VMEM((count, GROUPS, PAPERS, width), BF16),
@@ -664,33 +642,28 @@
             pltpu.VMEM((METAS, PAPERS, width), BF16),
             pltpu.VMEM((PAPERS, 256), BF16),
             pltpu.VMEM((PAPERS, side), BF16),
-            pltpu.VMEM((GROUPS, PAPERS, 256), BF16),
-            pltpu.VMEM((GROUPS, PAPERS, 256), BF16),
+            pltpu.VMEM((GROUPS, PAPERS, 512), BF16),
+            pltpu.VMEM((GROUPS, PAPERS, 512), BF16),
             pltpu.VMEM((METAS, PAPERS, mixed), BF16),
-            pltpu.VMEM((count, batch, mixed), BF16),
+            pltpu.VMEM((count, batch, width), BF16),
             pltpu.VMEM((2, GROUPS, CHIPS, META_ROWS, 128), BF16),
             pltpu.VMEM((GROUPS, CHIPS, META_ROWS, 128), BF16),
             pltpu.VMEM((GROUPS, CHIPS, META_ROWS, 128), BF16),
             pltpu.VMEM((CHIPS, META_ROWS, 128), BF16),
             pltpu.VMEM((CHIPS, META_ROWS, 128), BF16),
-            pltpu.VMEM((2, CHIPS, GROUPS, half - META_ROWS, 128), BF16),
-            pltpu.VMEM((CHIPS, GROUPS, half - META_ROWS, 128), BF16),
-            pltpu.VMEM((CHIPS, GROUPS, half - META_ROWS, 128), BF16),
-            pltpu.VMEM((GROUPS, half - META_ROWS, 128), BF16),
-            pltpu.VMEM((GROUPS, half - META_ROWS, 128), BF16),
-            pltpu.VMEM((2, CHIPS, part_rows, mixed), BF16),
-            pltpu.VMEM((CHIPS, part_rows, mixed), BF16),
-            pltpu.VMEM((CHIPS, part_rows, mixed), BF16),
-            pltpu.VMEM((GROUPS, part_rows, mixed), BF16),
+            pltpu.VMEM((2, CHIPS, GROUPS * node_rows + qv_rows, 128), BF16),
+            pltpu.VMEM((CHIPS, GROUPS * node_rows + qv_rows, 128), BF16),
+            pltpu.VMEM((CHIPS, GROUPS * node_rows + qv_rows, 128), BF16),
+            pltpu.VMEM((GROUPS, node_rows + qv_rows, 128), BF16),
+            pltpu.VMEM((GROUPS, node_rows + qv_rows, 128), BF16),
             pltpu.VMEM((count, 2, CHIPS, part, width), BF16),
             pltpu.VMEM((count, CHIPS, part, width), BF16),
             pltpu.VMEM((count, CHIPS, part, width), BF16),
             pltpu.VMEM((2, 8, 128), F32),
-            pltpu.VMEM((GROUPS, 8, 128), F32),
             pltpu.SemaphoreType.DMA((GROUPS, 4)),
             pltpu.SemaphoreType.DMA((GROUPS, 4)),
-            pltpu.SemaphoreType.DMA((GROUPS, 4)),
-            pltpu.SemaphoreType.DMA((GROUPS, 4)),
+            pltpu.SemaphoreType.DMA((GROUPS, 2)),
+            pltpu.SemaphoreType.DMA((GROUPS, 2)),
             pltpu.SemaphoreType.DMA((16, 8)),
             pltpu.SemaphoreType.DMA((16, 8)),
             pltpu.SemaphoreType.DMA((8,)),
@@ -711,15 +684,13 @@
             jax.ShapeDtypeStruct((class_count, count * width), F32),
             jax.ShapeDtypeStruct((1, 1), F32),
         ),
-        in_specs=[anywhere] * 4,
+        in_specs=[anywhere] * 2,
         out_specs=(anywhere,) + (vmem,) * 3 + (pl.BlockSpec(memory_space=pltpu.SMEM),),
         scratch_shapes=[
             pltpu.VMEM((count, 2, CHIPS, part, width), BF16),
-            pltpu.VMEM((2, CHIPS, half, 128), BF16),
-            pltpu.VMEM((2, CHIPS, part_rows, mixed), BF16),
-            pltpu.VMEM((2, CHIPS, 8, 128), F32),
+            pltpu.VMEM((2, CHIPS, fin_rows, 128), BF16),
             pltpu.VMEM((count, feat, width), F32),
-            pltpu.SemaphoreType.DMA((5,)),
+            pltpu.SemaphoreType.DMA((3,)),
             pltpu.SemaphoreType.DMA((2,)),
         ],
         compiler_params=pltpu.CompilerParams(vmem_limit_bytes=62 * 1024 * 1024),

time: 133 us -> 136 us (1.023)
  Pallas kernels: 132 us -> 135 us
    pallas_call x1, Pallas kernels: 128 us -> 131 us  [local(): pl.pallas_call(functools.partial(step_kernel, 1.0 / batch_total ** 0.5, c...]
where the time goes in v5:
time: 136 us
  Pallas kernels  135 us (99%)
    pallas_call x1, Pallas kernels, local(): pl.pallas_call(functools.partial(step_kernel, 1.0 / batch_total ** 0.5, c...  131 us
    pallas_call x1, Pallas kernels, local(): pl.pallas_call(functools.partial(finish_kernel, batch_total, class_count)...  4.22 us

profile of v5, /device:TPU:1, one launch (start us, length us, event | category | flops | bytes accessed | tf_op | source)
XLA Modules:
  0.0 135.9 jit_solution(1762995926519656018)
XLA Ops:
  0.6 130.9 %shard_map.110 = (bf16[2,2,8,48,512]{4,3,2,1,0:T(8,128)(2,1)}, bf16[2,8,240,128]{3,2,1,0:T(8,128)(2,1)}) custom-call(s32[12,128]{1,0:T(8,128)} %bitcast.3, s32[12,128]{1,0:T(8,128)} %bitcast.4, bf16[2,2048,768]{2,1,0:T(8,128)(2,1)} %agg_hbm.1, bf16[2,768,512]{2,1,0:T(8,128)(2,1)} %w_proj_hbm.1, bf16[512,128]{1,0:T(8,128)(2,1)} %w_qk_hbm.1, ...), custom_call_target="tpu_custom_call" | custom-call | tf_op jit(solution)/shard_map/pallas_call | solution.py:624
  131.6 4.2 %shard_map.111 = (f32[2,768,512]{2,1,0:T(8,128)}, f32[512,128]{1,0:T(8,128)}, f32[512,512]{1,0:T(8,128)}, f32[153,1024]{1,0:T(8,128)}, f32[1,1]{1,0:T(1,128)}) custom-call(bf16[2,2,8,48,512]{4,3,2,1,0:T(8,128)(2,1)} %get-tuple-element.12.gp_hbm, bf16[2,8,240,128]{3,2,1,0:T(8,128)(2,1)} %get-tuple-element.13.fin_hbm), custom_call_target="tpu_custom_call" | custom-call | tf_op jit(solution)/shard_map/pallas_call | solution.py:678

commit v6 on v4

--- a/solution.py
+++ b/solution.py
@@ -231,6 +231,13 @@
             for m in range(2):
                 in_copy(g, h, m).wait_recv()
 
+        @pl.when(h == 1)
+        def _():
+            for g in groups:
+                mail_to(g, 0).start()
+            for g in groups:
+                keys_to(g, 0).start()
+
         def forward(t, c):
             b = h * (HALF // BLOCK) + t
             at = pl.ds(pl.multiple_of(b * BLOCK, BLOCK), BLOCK)
@@ -277,8 +284,11 @@
             box = mail_in if j == 0 else mail
             box[g, part(h), :128] = dl[:, :128]
             box[g, part(h), 128:] = second
-            if j:
-                mail_to(g, h).start()
+
+        @pl.when(h == 1)
+        def _():
+            for g in groups:
+                mail_to(g, 1).start()
 
         def spread(m, c):
             d_joined[m, part(h), :] = dot(dl[:, :CLASS_PAD], class_rows(m)).astype(BF16)
@@ -302,8 +312,12 @@
             return c
 
         lax.fori_loop(0, HALF // BLOCK, backward, 0, unroll=UNROLL)
-        for g in groups:
-            keys_to(g, h).start()
+
+        @pl.when(h == 1)
+        def _():
+            for g in groups:
+                keys_to(g, 1).start()
+
         for m in range(2):
             d_vk[m, key_rows(me, h), width:] = d_vq[2 * me + m, part(h), width:]
         return carry

time: 133 us -> 132 us (level)
    pallas_call x1, Pallas kernels: 128 us -> 126 us  [local(): pl.pallas_call(functools.partial(step_kernel, 1.0 / batch_total ** 0.5, c...]
where the time goes in v6:
time: 132 us; the launch traced here: 131 us
  Pallas kernels  131 us (99%)
    pallas_call x1, Pallas kernels, local(): pl.pallas_call(functools.partial(step_kernel, 1.0 / batch_total ** 0.5, c...  126 us
    pallas_call x1, Pallas kernels, local(): pl.pallas_call(functools.partial(finish_kernel, batch_total, class_count)...  4.23 us

profile of v6, /device:TPU:1, one launch (start us, length us, event | category | flops | bytes accessed | tf_op | source)
XLA Modules:
  0.0 131.5 jit_solution(3897286754310432340)
XLA Ops:
  0.6 126.4 %shard_map.110 = (bf16[2,2,8,48,512]{4,3,2,1,0:T(8,128)(2,1)}, bf16[2,8,80,128]{3,2,1,0:T(8,128)(2,1)}, bf16[2,8,32,640]{3,2,1,0:T(8,128)(2,1)}, f32[2,8,8,128]{3,2,1,0:T(8,128)}) custom-call(s32[12,128]{1,0:T(8,128)} %bitcast.3, s32[12,128]{1,0:T(8,128)} %bitcast.4, bf16[2,2048,768]{2,1,0:T(8,128)(2,1)} %agg_hbm.1, bf16[2,768,512]{2,1,0:T(8,128)(2,1)} %w_proj_hbm.1, ...), custom_call_target="tpu_custom_call" | custom-call | tf_op jit(solution)/shard_map/pallas_call | solution.py:658
  127.1 4.2 %shard_map.111 = (f32[2,768,512]{2,1,0:T(8,128)}, f32[512,128]{1,0:T(8,128)}, f32[512,512]{1,0:T(8,128)}, f32[153,1024]{1,0:T(8,128)}, f32[1,1]{1,0:T(1,128)}) custom-call(bf16[2,2,8,48,512]{4,3,2,1,0:T(8,128)(2,1)} %get-tuple-element.14.gp_hbm, bf16[2,8,80,128]{3,2,1,0:T(8,128)(2,1)} %get-tuple-element.15.cls_hbm, ...), custom_call_target="tpu_custom_call" | custom-call | tf_op jit(solution)/shard_map/pallas_call | solution.py:719

commit v7 on v6

--- a/solution.py
+++ b/solution.py
@@ -226,7 +226,7 @@
         here = d_vk.at[:, key_rows(g, h), pl.ds(width, 2 * KEY)]
         return remote(here, here, mail_send.at[g, 2 + h], mail_recv.at[g, 2 + h], {"meta": g})
 
-    def head(values, attention, kq, h, carry):
+    def head(values, attention, qk, kq, h, carry):
         for g in groups:
             for m in range(2):
                 in_copy(g, h, m).wait_recv()
@@ -238,17 +238,24 @@
             for g in groups:
                 keys_to(g, 0).start()
 
+        def mix(t, c):
+            metas = pl.ds(4 * t, 4)
+            mixed = dot(hidden[metas, part(h), :].reshape(4 * HALF, width), w_all[...]).astype(BF16)
+            mixed = mixed.reshape(4, HALF, width + 4 * KEY)
+            values[metas, part(h), :] = mixed[:, :, :width]
+            qk[metas, part(h), :] = mixed[:, :, width : width + 2 * KEY]
+            kq[metas, part(h), :] = mixed[:, :, width + 2 * KEY :]
+            return c
+
+        lax.fori_loop(0, METAS // 4, mix, 0, unroll=2)
+
         def forward(t, c):
             b = h * (HALF // BLOCK) + t
             at = pl.ds(pl.multiple_of(b * BLOCK, BLOCK), BLOCK)
             here = hidden[:, at, :].reshape(side, width)
-            mixed = dot(here, w_all[...]).astype(BF16)
-            v = mixed[:, :width]
-            swapped = mixed[:, width + 2 * KEY :]
-            values[b] = v
-            kq[b] = swapped
-            q = jnp.where(first, mixed[:, width : width + 2 * KEY].astype(F32), 0.0).astype(BF16)
-            scores = dot_nt(q, swapped) * scale
+            v = values[:, at, :].reshape(side, width)
+            q = jnp.where(first, qk[:, at, :].reshape(side, 2 * KEY).astype(F32), 0.0).astype(BF16)
+            scores = dot_nt(q, kq[:, at, :].reshape(side, 2 * KEY)) * scale
             weights = jnp.where(same, jnp.exp(scores), 0.0)
             att = weights * (1.0 / jnp.sum(weights, axis=1, keepdims=True))
             attention[b] = att
@@ -266,6 +273,7 @@
             METAS,
             lambda m, t: t + dot_nt(joined[m, part(h), :], class_rows_wide(m)),
             jnp.zeros((HALF, 256), F32),
+            unroll=8,
         )
         class_at = iota((HALF, 256), 1)
         exps = jnp.where(class_at < class_count, jnp.exp(logits), 0.0)
@@ -294,17 +302,17 @@
             d_joined[m, part(h), :] = dot(dl[:, :CLASS_PAD], class_rows(m)).astype(BF16)
             return c
 
-        lax.fori_loop(0, METAS, spread, 0)
+        lax.fori_loop(0, METAS, spread, 0, unroll=8)
 
         def backward(t, c):
             b = h * (HALF // BLOCK) + t
             at = pl.ds(pl.multiple_of(b * BLOCK, BLOCK), BLOCK)
             dj = d_joined[:, at, :].reshape(side, width)
             att = attention[b]
-            d_att = dot_nt(dj, values[b])
+            d_att = dot_nt(dj, values[:, at, :].reshape(side, width))
             mean = jnp.sum(att * d_att, axis=1, keepdims=True)
             d_scores = (att * (d_att - mean) * scale).astype(BF16)
-            swapped = kq[b]
+            swapped = kq[:, at, :].reshape(side, 2 * KEY)
             grad = jnp.where(first, dot(d_scores, swapped), dot_tn(d_scores, swapped))
             d_vq[:, at, width:] = grad.astype(BF16).reshape(METAS, BLOCK, 2 * KEY)
             d_val = dot_tn(att.astype(BF16), dj)
@@ -328,9 +336,10 @@
     blocks = PAPERS // BLOCK
     pl.run_scoped(
         heads,
-        pltpu.VMEM((blocks, side, width), BF16),
+        pltpu.VMEM((METAS, PAPERS, width), BF16),
         pltpu.VMEM((blocks, side, side), F32),
-        pltpu.VMEM((blocks, side, 2 * KEY), BF16),
+        pltpu.VMEM((METAS, PAPERS, 2 * KEY), BF16),
+        pltpu.VMEM((METAS, PAPERS, 2 * KEY), BF16),
     )
 
     def classes(g, carry):
@@ -344,7 +353,7 @@
                     cy[p, 4 * m + q, g] = grad[top + META_ROWS : top + CLASS_PAD // 2, lanes]
         return carry
 
-    lax.fori_loop(0, GROUPS, classes, 0)
+    lax.fori_loop(0, GROUPS, classes, 0, unroll=4)
     c0 = [to_sibling(0, cx.at[other], cx_in), to_sibling(7, cy.at[other], cy_in)]
     for copy in c0:
         copy.start()
@@ -370,7 +379,7 @@
         cy_in[g] = (cy[core, g].astype(F32) + cy_in[g].astype(F32)).astype(BF16)
         return carry
 
-    lax.fori_loop(0, GROUPS, pair_class, 0)
+    lax.fori_loop(0, GROUPS, pair_class, 0, unroll=4)
     for k in chips:
         to_chip(0, k, cy_in.at[k], cy_chip.at[chip]).start()
     for g in groups:
@@ -384,7 +393,7 @@
         qv_in[k] = (qv[core, k].astype(F32) + qv_in[k].astype(F32)).astype(BF16)
         return carry
 
-    lax.fori_loop(0, CHIPS, pair_qv, 0)
+    lax.fori_loop(0, CHIPS, pair_qv, 0, unroll=4)
     for k in chips:
         to_chip(2, k, qv_in.at[k], qv_chip.at[chip]).start()
     qv_chip[chip] = qv_in[chip]
@@ -437,7 +446,7 @@
             d_hidden[pl.ds(GROUPS * m + 2 * r, 2)] = grad.astype(BF16).reshape(2, PAPERS, width)
             return carry
 
-        lax.fori_loop(0, GROUPS // 2, some, 0)
+        lax.fori_loop(0, GROUPS // 2, some, 0, unroll=4)
 
     part_feat = gp.shape[3]
 
@@ -453,7 +462,7 @@
             gp_in[m, k] = (gp[m, core, k].astype(F32) + gp_in[m, k].astype(F32)).astype(BF16)
             return carry
 
-        lax.fori_loop(0, CHIPS, one, 0)
+        lax.fori_loop(0, CHIPS, one, 0, unroll=4)
         for k in chips:
             to_chip(9 + m, k, gp_in.at[m, k], gp_chip.at[m, chip]).start()
         gp_chip[m, chip] = gp_in[m, chip]
@@ -503,7 +512,7 @@
         cy_sum[g] = jnp.sum(cy_chip[:, g].astype(F32), axis=0).astype(BF16)
         return carry
 
-    lax.fori_loop(0, GROUPS, chip_sum, 0)
+    lax.fori_loop(0, GROUPS, chip_sum, 0, unroll=4)
     for g in groups:
         to_group(15, g, cy_sum.at[g], cy_meta.at[me]).start()
     cy_meta[me] = cy_sum[me]
@@ -527,7 +536,7 @@
         cx_sum[k] = jnp.sum(cx_meta[:, k].astype(F32), axis=0).astype(BF16)
         return carry
 
-    lax.fori_loop(0, CHIPS, meta_sum, 0)
+    lax.fori_loop(0, CHIPS, meta_sum, 0, unroll=4)
     for k in chips:
         to_chip(3, k, cx_sum.at[k], cx_chip.at[chip]).start()
     cx_chip[chip] = cx_sum[chip]

time: 132 us -> 139 us (1.053)
  Pallas kernels: 131 us -> 138 us
    pallas_call x1, Pallas kernels: 126 us -> 133 us  [local(): pl.pallas_call(functools.partial(step_kernel, 1.0 / batch_total ** 0.5, c...]
where the time goes in v7:
time: 139 us
  Pallas kernels  138 us (99%)
    pallas_call x1, Pallas kernels, local(): pl.pallas_call(functools.partial(step_kernel, 1.0 / batch_total ** 0.5, c...  133 us
    pallas_call x1, Pallas kernels, local(): pl.pallas_call(functools.partial(finish_kernel, batch_total, class_count)...  4.23 us

profile of v7, /device:TPU:1, one launch (start us, length us, event | category | flops | bytes accessed | tf_op | source)
XLA Modules:
  0.0 138.5 jit_solution(16983396158788404403)
XLA Ops:
  0.6 133.5 %shard_map.110 = (bf16[2,2,8,48,512]{4,3,2,1,0:T(8,128)(2,1)}, bf16[2,8,80,128]{3,2,1,0:T(8,128)(2,1)}, bf16[2,8,32,640]{3,2,1,0:T(8,128)(2,1)}, f32[2,8,8,128]{3,2,1,0:T(8,128)}) custom-call(s32[12,128]{1,0:T(8,128)} %bitcast.3, s32[12,128]{1,0:T(8,128)} %bitcast.4, bf16[2,2048,768]{2,1,0:T(8,128)(2,1)} %agg_hbm.1, bf16[2,768,512]{2,1,0:T(8,128)(2,1)} %w_proj_hbm.1, ...), custom_call_target="tpu_custom_call" | custom-call | tf_op jit(solution)/shard_map/pallas_call | solution.py:667
  134.1 4.2 %shard_map.111 = (f32[2,768,512]{2,1,0:T(8,128)}, f32[512,128]{1,0:T(8,128)}, f32[512,512]{1,0:T(8,128)}, f32[153,1024]{1,0:T(8,128)}, f32[1,1]{1,0:T(1,128)}) custom-call(bf16[2,2,8,48,512]{4,3,2,1,0:T(8,128)(2,1)} %get-tuple-element.14.gp_hbm, bf16[2,8,80,128]{3,2,1,0:T(8,128)(2,1)} %get-tuple-element.15.cls_hbm, ...), custom_call_target="tpu_custom_call" | custom-call | tf_op jit(solution)/shard_map/pallas_call | solution.py:728

commit v8 on v6

--- a/solution.py
+++ b/solution.py
@@ -19,7 +19,7 @@
 KEY = 64
 CLASS_PAD = 160
 TAIL = CLASS_PAD - 128
-META_ROWS = 48
+META_ROWS = 64
 UNROLL = 6
 
 
@@ -370,7 +370,7 @@
         cy_in[g] = (cy[core, g].astype(F32) + cy_in[g].astype(F32)).astype(BF16)
         return carry
 
-    lax.fori_loop(0, GROUPS, pair_class, 0)
+    lax.fori_loop(0, GROUPS, pair_class, 0, unroll=4)
     for k in chips:
         to_chip(0, k, cy_in.at[k], cy_chip.at[chip]).start()
     for g in groups:
@@ -384,7 +384,7 @@
         qv_in[k] = (qv[core, k].astype(F32) + qv_in[k].astype(F32)).astype(BF16)
         return carry
 
-    lax.fori_loop(0, CHIPS, pair_qv, 0)
+    lax.fori_loop(0, CHIPS, pair_qv, 0, unroll=4)
     for k in chips:
         to_chip(2, k, qv_in.at[k], qv_chip.at[chip]).start()
     qv_chip[chip] = qv_in[chip]
@@ -437,7 +437,7 @@
             d_hidden[pl.ds(GROUPS * m + 2 * r, 2)] = grad.astype(BF16).reshape(2, PAPERS, width)
             return carry
 
-        lax.fori_loop(0, GROUPS // 2, some, 0)
+        lax.fori_loop(0, GROUPS // 2, some, 0, unroll=4)
 
     part_feat = gp.shape[3]
 
@@ -453,7 +453,7 @@
             gp_in[m, k] = (gp[m, core, k].astype(F32) + gp_in[m, k].astype(F32)).astype(BF16)
             return carry
 
-        lax.fori_loop(0, CHIPS, one, 0)
+        lax.fori_loop(0, CHIPS, one, 0, unroll=4)
         for k in chips:
             to_chip(9 + m, k, gp_in.at[m, k], gp_chip.at[m, chip]).start()
         gp_chip[m, chip] = gp_in[m, chip]
@@ -503,7 +503,7 @@
         cy_sum[g] = jnp.sum(cy_chip[:, g].astype(F32), axis=0).astype(BF16)
         return carry
 
-    lax.fori_loop(0, GROUPS, chip_sum, 0)
+    lax.fori_loop(0, GROUPS, chip_sum, 0, unroll=4)
     for g in groups:
         to_group(15, g, cy_sum.at[g], cy_meta.at[me]).start()
     cy_meta[me] = cy_sum[me]
@@ -527,7 +527,7 @@
         cx_sum[k] = jnp.sum(cx_meta[:, k].astype(F32), axis=0).astype(BF16)
         return carry
 
-    lax.fori_loop(0, CHIPS, meta_sum, 0)
+    lax.fori_loop(0, CHIPS, meta_sum, 0, unroll=4)
     for k in chips:
         to_chip(3, k, cx_sum.at[k], cx_chip.at[chip]).start()
     cx_chip[chip] = cx_sum[chip]

time: 132 us -> 131 us (level)
  no operation moved by 1% of the time
where the time goes in v8:
time: 131 us
  Pallas kernels  130 us (99%)
    pallas_call x1, Pallas kernels, local(): pl.pallas_call(functools.partial(step_kernel, 1.0 / batch_total ** 0.5, c...  126 us
    pallas_call x1, Pallas kernels, local(): pl.pallas_call(functools.partial(finish_kernel, batch_total, class_count)...  4.23 us

profile of v8, /device:TPU:1, one launch (start us, length us, event | category | flops | bytes accessed | tf_op | source)
XLA Modules:
  0.0 130.8 jit_solution(9444249177991370140)
XLA Ops:
  0.6 125.7 %shard_map.110 = (bf16[2,2,8,48,512]{4,3,2,1,0:T(8,128)(2,1)}, bf16[2,8,80,128]{3,2,1,0:T(8,128)(2,1)}, bf16[2,8,32,640]{3,2,1,0:T(8,128)(2,1)}, f32[2,8,8,128]{3,2,1,0:T(8,128)}) custom-call(s32[12,128]{1,0:T(8,128)} %bitcast.3, s32[12,128]{1,0:T(8,128)} %bitcast.4, bf16[2,2048,768]{2,1,0:T(8,128)(2,1)} %agg_hbm.1, bf16[2,768,512]{2,1,0:T(8,128)(2,1)} %w_proj_hbm.1, ...), custom_call_target="tpu_custom_call" | custom-call | tf_op jit(solution)/shard_map/pallas_call | solution.py:658
  126.3 4.2 %shard_map.111 = (f32[2,768,512]{2,1,0:T(8,128)}, f32[512,128]{1,0:T(8,128)}, f32[512,512]{1,0:T(8,128)}, f32[153,1024]{1,0:T(8,128)}, f32[1,1]{1,0:T(1,128)}) custom-call(bf16[2,2,8,48,512]{4,3,2,1,0:T(8,128)(2,1)} %get-tuple-element.14.gp_hbm, bf16[2,8,80,128]{3,2,1,0:T(8,128)(2,1)} %get-tuple-element.15.cls_hbm, ...), custom_call_target="tpu_custom_call" | custom-call | tf_op jit(solution)/shard_map/pallas_call | solution.py:719
